TPU v7x, 32 devices: a whole 2x2x4 slice. The times are simulated.
32 devices in a mesh: groups: 2 (over y), nodes: 16 (over z, x, core).
Axes of the slice: x: 2, y: 2, z: 4, core: 2. Of those that a mesh axis runs over, the one named last changes fastest.
Arguments:
- grid_latents: bfloat16 [32768, 1024], P(('groups', 'nodes')), parts along dimension 0, may hold values from -16 to 16
- mesh_latents: bfloat16 [8192, 1024], P(('groups', 'nodes')), parts along dimension 0, may hold values from -16 to 16
- neighbour_tiles: int32 [32, 6], P('nodes'), may hold values from 0 to 127, as said below
- neighbour_live: int32 [32, 6], P('nodes'), may hold values from 0 to 1, as said below
- w_query: bfloat16 [1024, 1024], replicated, may hold values from -0.1875 to 0.1875
- w_keyval: bfloat16 [1024, 2048], replicated, may hold values from -0.1875 to 0.1875
- w_out: bfloat16 [1024, 1024], replicated, may hold values from -0.375 to 0.375
Outputs:
- mesh_next: float32 [8192, 1024], P(('groups', 'nodes')), parts along dimension 0
There are 2 independent parts, one for each index of `groups`. A program takes and returns all parts, laid end to end along the dimension named above; an argument that names none is the same for every part. Nothing has to cross between parts.
Inputs may be any that keep to these rules, and one draw needn't show every extreme that they name: `neighbour_tiles`: tile t lies on device t // 8 along nodes and mesh tile m on device m // 2; every listed tile lies on a device at most 2 indices away cyclically. The 6 entries of one mesh tile are distinct. Among the live entries of one device's mesh tiles at most 2 distinct tiles come from any one other device, and on every device some other device gives exactly 2. `neighbour_live`: each mesh tile has 2 to 6 live entries.
All inputs are finite; a program needn't handle non-finite values.
Results may differ from a plain program's by a relative error of at most 0.002.
The roundings to bfloat16 on the way count: a program that leaves them out, or rounds other values in their place, can miss the bound.
Values may be sent and summed in bfloat16 or wider, within the bound.
A program may use at most 128 MiB of HBM per device.

v0:
```python
import jax
import jax.numpy as jnp
from jax import lax
from jax.sharding import PartitionSpec as P

HEADS = 16
TILE = 128
REACH = 2
CAP = 2


def from_behind(block, axis, distance):
    devices = range(lax.axis_size(axis))
    route = [((i - distance) % len(devices), i) for i in devices]
    return lax.ppermute(block, axis, route)


def fetch(block, offset):
    return from_behind(block, "nodes", -offset)


def pick_tile(sources, source_index, local_index):
    picked = lax.dynamic_index_in_dim(sources[0], local_index, 0, keepdims=False)
    for number in range(1, len(sources)):
        other = lax.dynamic_index_in_dim(sources[number], local_index, 0, keepdims=False)
        picked = jnp.where(source_index == number, other, picked)
    return picked


def attend_one(query_tile, slot_tiles, live_row):
    tile_rows, model_width = query_tile.shape
    head_size = model_width // HEADS
    query_heads = query_tile.reshape(tile_rows, HEADS, head_size)
    score_blocks = []
    value_blocks = []
    for slot, tile in enumerate(slot_tiles):
        key_heads = tile[:, :model_width].reshape(tile_rows, HEADS, head_size)
        value_blocks.append(tile[:, model_width:].reshape(tile_rows, HEADS, head_size))
        block = jnp.einsum(
            "qhd,khd->hqk", query_heads, key_heads, preferred_element_type=jnp.float32
        )
        block = block * head_size ** (-0.5)
        score_blocks.append(jnp.where(live_row[slot] > 0, block, -1e30))
    scores = jnp.concatenate(score_blocks, axis=-1)
    row_top = jnp.max(scores, axis=-1, keepdims=True)
    raised = jnp.exp(scores - row_top)
    row_total = jnp.sum(raised, axis=-1, keepdims=True)
    weights = (raised / row_total).astype(jnp.bfloat16)
    mixture = jnp.zeros((tile_rows, HEADS, head_size), jnp.float32)
    for slot, values in enumerate(value_blocks):
        part_weights = weights[:, :, slot * tile_rows : (slot + 1) * tile_rows]
        mixture = mixture + jnp.einsum(
            "hqk,khd->qhd", part_weights, values, preferred_element_type=jnp.float32
        )
    return mixture.astype(jnp.bfloat16).reshape(tile_rows, model_width)


def per_device(
    grid_latents, mesh_latents, neighbour_tiles, neighbour_live, w_query, w_keyval, w_out
):
    model_width = w_query.shape[0]
    tile_rows = TILE
    own_tiles = grid_latents.shape[0] // tile_rows
    mesh_tiles = mesh_latents.shape[0] // tile_rows
    node_count = lax.axis_size("nodes")
    position = lax.axis_index("nodes")
    offsets = [shift_by for shift_by in range(-REACH, REACH + 1) if shift_by != 0]
    payload = jnp.dot(grid_latents, w_keyval, preferred_element_type=jnp.float32).astype(
        jnp.bfloat16
    )
    payload = payload.reshape(own_tiles, tile_rows, 2 * model_width)
    tile_owner = neighbour_tiles // own_tiles
    tile_local = neighbour_tiles % own_tiles
    tile_offset = (tile_owner - position + node_count + REACH) % node_count - REACH
    source_index = jnp.zeros(neighbour_tiles.shape, jnp.int32)
    local_index = jnp.where(tile_offset == 0, tile_local, 0)
    received = []
    live_flag = neighbour_live > 0
    tile_ids = jnp.arange(own_tiles, dtype=jnp.int32)
    slot_ids = jnp.arange(CAP, dtype=jnp.int32)
    for offset_index, offset in enumerate(offsets):
        wanted = live_flag & (tile_offset == offset)
        needed = jnp.any(
            wanted[:, :, None] & (tile_local[:, :, None] == tile_ids[None, None, :]), axis=(0, 1)
        )
        placing = jnp.cumsum(needed.astype(jnp.int32)) - 1
        chosen = needed[None, :] & (placing[None, :] == slot_ids[:, None])
        request = jnp.sum(jnp.where(chosen, tile_ids[None, :], 0), axis=1)
        requested = from_behind(request, "nodes", offset)
        received.append(fetch(jnp.take(payload, requested, axis=0), offset))
        source_index = jnp.where(wanted, offset_index + 1, source_index)
        local_index = jnp.where(wanted, jnp.take(placing, tile_local), local_index)
    sources = [payload] + received
    queries = jnp.dot(mesh_latents, w_query, preferred_element_type=jnp.float32).astype(
        jnp.bfloat16
    )
    queries = queries.reshape(mesh_tiles, tile_rows, model_width)
    outputs = []
    for mesh_tile in range(mesh_tiles):
        slot_tiles = [
            pick_tile(sources, source_index[mesh_tile, slot], local_index[mesh_tile, slot])
            for slot in range(neighbour_tiles.shape[1])
        ]
        outputs.append(attend_one(queries[mesh_tile], slot_tiles, neighbour_live[mesh_tile]))
    attended = jnp.concatenate(outputs, axis=0)
    return mesh_latents.astype(jnp.float32) + jnp.dot(
        attended, w_out, preferred_element_type=jnp.float32
    )


def solution(mesh):
    return jax.shard_map(
        per_device,
        mesh=mesh,
        in_specs=(
            P(("groups", "nodes"), None),
            P(("groups", "nodes"), None),
            P("nodes", None),
            P("nodes", None),
            P(),
            P(),
            P(),
        ),
        out_specs=P(("groups", "nodes"), None),
        check_vma=False,
    )
```

profile of v0, /device:TPU:0, one launch (start us, length us, event | category | flops | bytes accessed | tf_op | source)
XLA Modules:
  0.0 202.1 jit_solution(4292983124530878410)
XLA Ops:
  1.3 5.5 %collective-permute-start.4 = (s32[2]{0:T(128)S(1)}, s32[2]{0:T(128)S(1)}, u32[]{:S(2)}, u32[]{:S(2)}) collective-permute-start(s32[2]{0:T(128)S(1)} %fusion.48), channel_id=1, source_target_pairs={{1,0},{2,1},{3,2},{4,3},{5,4},{6,5},{7,6},{8,7},{9,8},{10,9},{11,1... | collective-permute-start | bytes 32 | tf_op jit(solution)/shard_map/ppermute | solution.py:15
  13.0 8.2 %convolution_convert_fusion = bf16[1024,2048]{1,0:T(8,128)(2,1)} fusion(bf16[1024,1024]{1,0:T(8,128)(2,1)S(1)} %copy-done, bf16[1024,2048]{1,0:T(8,128)(2,1)} %param.16), kind=kOutput, calls=%fused_computation.14 | convolution fusion | flops 4297064448 | bytes 10485760 | tf_op jit(solution)/shard_map/dot_general | solution.py:68
  21.2 3.8 %gather_fusion.7 = bf16[2,128,2048]{2,1,0:T(8,128)(2,1)} fusion(bf16[8,128,2048]{2,1,0:T(8,128)(2,1)} %bitcast.186, s32[1024]{0:T(1024)S(1)} %pad_clamp_fusion), kind=kCustom, calls=%fused_computation.4.clone | custom fusion | bytes 2097160 | tf_op jit(solution)/shard_map/jit(_take)/gather | solution.py:90
  25.0 2.8 %gather_fusion.6 = bf16[2,128,2048]{2,1,0:T(8,128)(2,1)S(1)} fusion(bf16[8,128,2048]{2,1,0:T(8,128)(2,1)} %bitcast.187, s32[1024]{0:T(1024)S(1)} %pad_clamp_fusion.1), kind=kCustom, calls=%fused_computation.3.clone | custom fusion | bytes 2097160 | tf_op jit(solution)/shard_map/jit(_take)/gather | solution.py:90
  27.8 2.8 %gather_fusion.5 = bf16[2,128,2048]{2,1,0:T(8,128)(2,1)S(1)} fusion(bf16[8,128,2048]{2,1,0:T(8,128)(2,1)} %bitcast.188, s32[1024]{0:T(1024)S(1)} %pad_clamp_fusion.2), kind=kCustom, calls=%fused_computation.2.clone | custom fusion | bytes 2097160 | tf_op jit(solution)/shard_map/jit(_take)/gather | solution.py:90
  30.6 2.8 %gather_fusion = bf16[2,128,2048]{2,1,0:T(8,128)(2,1)S(1)} fusion(bf16[8,128,2048]{2,1,0:T(8,128)(2,1)} %bitcast.189, s32[1024]{0:T(1024)S(1)} %pad_clamp_fusion.4), kind=kCustom, calls=%fused_computation.clone | custom fusion | bytes 2097160 | tf_op jit(solution)/shard_map/jit(_take)/gather | solution.py:90
  34.6 3.5 %collective-permute-start.1 = (bf16[2,128,2048]{2,1,0:T(8,128)(2,1)}, bf16[2,128,2048]{2,1,0:T(8,128)(2,1)S(1)}, u32[]{:S(2)}, u32[]{:S(2)}) collective-permute-start(bf16[2,128,2048]{2,1,0:T(8,128)(2,1)} %broadcast_select_fusion.3), channel_id=1, source_target_pairs={{2,0},{3,1},{4,2},{5,3},{6,4},{7,5},{8,6},{9,7},{10,8},{11,9},{12,... | collective-permute-start | bytes 3145736 | tf_op jit(solution)/shard_map/ppermute | solution.py:15
  119.7 2.5 %convolution_convert_fusion.1 = bf16[256,1024]{1,0:T(8,128)(2,1)S(1)} fusion(bf16[256,1024]{1,0:T(8,128)(2,1)} %param.12, bf16[1024,1024]{1,0:T(8,128)(2,1)} %param.15), kind=kOutput, calls=%fused_computation.40 | convolution fusion | flops 537133056 | bytes 3145728 | tf_op jit(solution)/shard_map/dot_general | solution.py:94
  122.9 1.8 copy.95
  125.6 2.6 %select_bitcast_fusion.6 = (bf16[128,2048]{1,0:T(8,128)(2,1)S(1)}, bf16[128,2048]{1,0:T(8,128)(2,1)}) fusion(bf16[8,128,2048]{2,1,0:T(8,128)(2,1)} %bitcast.190, s32[]{:T(128)S(6)} %select_n.704, bf16[2,128,2048]{2,1,0:T(8,128)(2,1)} %collective-permute-done.7, s32[]{:T(128)S(6)} %select_n.700, bf16[2,128,2048]{2,1,0:T(8,128)(2,1)S(1)} %collective-permute-done.5, ...), kind=kLoop, calls=%fused_computation.80 | loop fusion | flops 2097152 | bytes 6291480 | tf_op jit(solution)/shard_map/jit(_where)/select_n | solution.py:26
  128.9 1.8 copy.111
  133.3 1.8 copy.130
  136.0 2.5 %select_bitcast_fusion.7 = (bf16[128,2048]{1,0:T(8,128)(2,1)S(1)}, bf16[128,2048]{1,0:T(8,128)(2,1)}) fusion(bf16[8,128,2048]{2,1,0:T(8,128)(2,1)} %bitcast.191, s32[]{:T(128)S(6)} %select_n.691, bf16[2,128,2048]{2,1,0:T(8,128)(2,1)} %collective-permute-done.7, s32[]{:T(128)S(6)} %select_n.687, bf16[2,128,2048]{2,1,0:T(8,128)(2,1)S(1)} %collective-permute-done.5, ...), kind=kLoop, calls=%fused_computation.81 | loop fusion | flops 2097152 | bytes 6291480 | tf_op jit(solution)/shard_map/jit(_where)/select_n | solution.py:26
  140.5 1.8 copy.100
  142.3 1.9 fusion.73
  144.2 1.8 copy.128
  145.9 1.8 copy.119
  147.7 2.5 %select_bitcast_fusion.8 = (bf16[128,2048]{1,0:T(8,128)(2,1)S(1)}, bf16[128,2048]{1,0:T(8,128)(2,1)}) fusion(bf16[8,128,2048]{2,1,0:T(8,128)(2,1)} %bitcast.192, s32[]{:T(128)S(6)} %select_n.678, bf16[2,128,2048]{2,1,0:T(8,128)(2,1)} %collective-permute-done.7, s32[]{:T(128)S(6)} %select_n.674, bf16[2,128,2048]{2,1,0:T(8,128)(2,1)S(1)} %collective-permute-done.5, ...), kind=kLoop, calls=%fused_computation.82 | loop fusion | flops 2097152 | bytes 6291480 | tf_op jit(solution)/shard_map/jit(_where)/select_n | solution.py:26
  151.1 1.8 copy.107
  152.9 1.8 copy.99
  154.7 1.9 fusion.74
  158.3 1.8 copy.118
  160.1 2.5 %select_bitcast_fusion.9 = (bf16[128,2048]{1,0:T(8,128)(2,1)S(1)}, bf16[128,2048]{1,0:T(8,128)(2,1)}) fusion(bf16[8,128,2048]{2,1,0:T(8,128)(2,1)} %bitcast.193, s32[]{:T(128)S(6)} %select_n.665, bf16[2,128,2048]{2,1,0:T(8,128)(2,1)} %collective-permute-done.7, s32[]{:T(128)S(6)} %select_n.661, bf16[2,128,2048]{2,1,0:T(8,128)(2,1)S(1)} %collective-permute-done.5, ...), kind=kLoop, calls=%fused_computation.83 | loop fusion | flops 2097152 | bytes 6291480 | tf_op jit(solution)/shard_map/jit(_where)/select_n | solution.py:26
  163.5 1.8 copy.105
  165.3 1.8 copy.98
  167.1 1.9 fusion.75
  169.0 1.8 copy.124
  170.8 1.8 copy.117
  172.6 2.6 %select_bitcast_fusion.10 = (bf16[128,2048]{1,0:T(8,128)(2,1)S(1)}, bf16[128,2048]{1,0:T(8,128)(2,1)}) fusion(bf16[8,128,2048]{2,1,0:T(8,128)(2,1)} %bitcast.194, s32[]{:T(128)S(6)} %select_n.652, bf16[2,128,2048]{2,1,0:T(8,128)(2,1)} %collective-permute-done.7, s32[]{:T(128)S(6)} %select_n.648, bf16[2,128,2048]{2,1,0:T(8,128)(2,1)S(1)} %collective-permute-done.5, ...), kind=kLoop, calls=%fused_computation.84 | loop fusion | flops 2097152 | bytes 6291480 | tf_op jit(solution)/shard_map/jit(_where)/select_n | solution.py:26
  176.0 1.8 copy.103
  177.8 2.5 %select_bitcast_fusion.11 = (bf16[128,2048]{1,0:T(8,128)(2,1)S(1)}, bf16[128,2048]{1,0:T(8,128)(2,1)}) fusion(bf16[8,128,2048]{2,1,0:T(8,128)(2,1)} %bitcast.195, s32[]{:T(128)S(6)} %select_n.638, bf16[2,128,2048]{2,1,0:T(8,128)(2,1)} %collective-permute-done.7, s32[]{:T(128)S(6)} %select_n.631, bf16[2,128,2048]{2,1,0:T(8,128)(2,1)S(1)} %collective-permute-done.5, ...), kind=kLoop, calls=%fused_computation.85 | loop fusion | flops 2097152 | bytes 6291480 | tf_op jit(solution)/shard_map/jit(_where)/select_n | solution.py:26
  182.1 1.8 copy.97
  (168 shorter events, 47.9 us)
Async XLA Ops:
  0.0 13.0 %copy-start = (bf16[1024,1024]{1,0:T(8,128)(2,1)S(1)}, bf16[1024,1024]{1,0:T(8,128)(2,1)}, u32[]{:S(2)}) copy-start(bf16[1024,1024]{1,0:T(8,128)(2,1)} %param.11) | copy-start | bytes 6291460
  1.3 19.8 %collective-permute-start.4 = (s32[2]{0:T(128)S(1)}, s32[2]{0:T(128)S(1)}, u32[]{:S(2)}, u32[]{:S(2)}) collective-permute-start(s32[2]{0:T(128)S(1)} %fusion.48), channel_id=1, source_target_pairs={{1,0},{2,1},{3,2},{4,3},{5,4},{6,5},{7,6},{8,7},{9,8},{10,9},{11,1... | collective-permute-start | bytes 32 | tf_op jit(solution)/shard_map/ppermute | solution.py:15
  7.1 14.1 %collective-permute-start.6 = (s32[2]{0:T(128)S(1)}, s32[2]{0:T(128)S(1)}, u32[]{:S(2)}, u32[]{:S(2)}) collective-permute-start(s32[2]{0:T(128)S(1)} %fusion.49), channel_id=1, source_target_pairs={{2,0},{3,1},{4,2},{5,3},{6,4},{7,5},{8,6},{9,7},{10,8},{11,9},{12,... | collective-permute-start | bytes 32 | tf_op jit(solution)/shard_map/ppermute | solution.py:15
  8.0 13.2 %collective-permute-start.2 = (s32[2]{0:T(128)S(1)}, s32[2]{0:T(128)S(1)}, u32[]{:S(2)}, u32[]{:S(2)}) collective-permute-start(s32[2]{0:T(128)S(1)} %fusion.47), channel_id=1, source_target_pairs={{15,0},{0,1},{1,2},{2,3},{3,4},{4,5},{5,6},{6,7},{7,8},{8,9},{9,10... | collective-permute-start | bytes 32 | tf_op jit(solution)/shard_map/ppermute | solution.py:15
  8.6 12.6 %collective-permute-start = (s32[2]{0:T(128)S(1)}, s32[2]{0:T(128)S(1)}, u32[]{:S(2)}, u32[]{:S(2)}) collective-permute-start(s32[2]{0:T(128)S(1)} %fusion.42), channel_id=1, source_target_pairs={{14,0},{15,1},{0,2},{1,3},{2,4},{3,5},{4,6},{5,7},{6,8},{7,9},{8,1... | collective-permute-start | bytes 32 | tf_op jit(solution)/shard_map/ppermute | solution.py:15
  27.8 83.9 %copy-start.28 = (s32[2,6]{1,0:T(2,128)S(1)}, s32[2,6]{1,0:T(2,128)}, u32[]{:S(2)}) copy-start(s32[2,6]{1,0:T(2,128)} %param.14) | copy-start | bytes 148
  33.5 8.0 %copy-start.2 = (bf16[2,128,2048]{2,1,0:T(8,128)(2,1)S(1)}, bf16[2,128,2048]{2,1,0:T(8,128)(2,1)}, u32[]{:S(2)}) copy-start(bf16[2,128,2048]{2,1,0:T(8,128)(2,1)} %gather_fusion.7) | copy-start | bytes 3145732
  34.6 91.0 %collective-permute-start.1 = (bf16[2,128,2048]{2,1,0:T(8,128)(2,1)}, bf16[2,128,2048]{2,1,0:T(8,128)(2,1)S(1)}, u32[]{:S(2)}, u32[]{:S(2)}) collective-permute-start(bf16[2,128,2048]{2,1,0:T(8,128)(2,1)} %broadcast_select_fusion.3), channel_id=1, source_target_pairs={{2,0},{3,1},{4,2},{5,3},{6,4},{7,5},{8,6},{9,7},{10,8},{11,9},{12,... | collective-permute-start | bytes 3145736 | tf_op jit(solution)/shard_map/ppermute | solution.py:15
  39.3 86.3 %collective-permute-start.3 = (bf16[2,128,2048]{2,1,0:T(8,128)(2,1)}, bf16[2,128,2048]{2,1,0:T(8,128)(2,1)S(1)}, u32[]{:S(2)}, u32[]{:S(2)}) collective-permute-start(bf16[2,128,2048]{2,1,0:T(8,128)(2,1)} %broadcast_select_fusion.2), channel_id=1, source_target_pairs={{1,0},{2,1},{3,2},{4,3},{5,4},{6,5},{7,6},{8,7},{9,8},{10,9},{11,1... | collective-permute-start | bytes 3145736 | tf_op jit(solution)/shard_map/ppermute | solution.py:15
  41.4 84.2 %collective-permute-start.5 = (bf16[2,128,2048]{2,1,0:T(8,128)(2,1)}, bf16[2,128,2048]{2,1,0:T(8,128)(2,1)S(1)}, u32[]{:S(2)}, u32[]{:S(2)}) collective-permute-start(bf16[2,128,2048]{2,1,0:T(8,128)(2,1)} %broadcast_select_fusion.1), channel_id=1, source_target_pairs={{15,0},{0,1},{1,2},{2,3},{3,4},{4,5},{5,6},{6,7},{7,8},{8,9},{9,10... | collective-permute-start | bytes 3145736 | tf_op jit(solution)/shard_map/ppermute | solution.py:15
  42.6 83.0 %collective-permute-start.7 = (bf16[2,128,2048]{2,1,0:T(8,128)(2,1)}, bf16[2,128,2048]{2,1,0:T(8,128)(2,1)}, u32[]{:S(2)}, u32[]{:S(2)}) collective-permute-start(bf16[2,128,2048]{2,1,0:T(8,128)(2,1)} %broadcast_select_fusion), channel_id=1, source_target_pairs={{14,0},{15,1},{0,2},{1,3},{2,4},{3,5},{4,6},{5,7},{6,8},{7,9},{8,1... | collective-permute-start | bytes 3145736 | tf_op jit(solution)/shard_map/ppermute | solution.py:15
  180.3 7.7 %copy-start.18 = (bf16[128,1024]{0,1:T(8,128)(2,1)S(1)}, bf16[128,1024]{0,1:T(8,128)(2,1)}, u32[]{:S(2)}) copy-start(bf16[128,1024]{0,1:T(8,128)(2,1)} %copy.114) | copy-start | bytes 786436
  180.3 8.5 %copy-start.25 = (bf16[128,1024]{0,1:T(8,128)(2,1)S(1)}, bf16[128,1024]{0,1:T(8,128)(2,1)}, u32[]{:S(2)}) copy-start(bf16[128,1024]{0,1:T(8,128)(2,1)} %copy.117) | copy-start | bytes 786436
  180.3 8.9 %copy-start.24 = (bf16[128,1024]{0,1:T(8,128)(2,1)S(1)}, bf16[128,1024]{0,1:T(8,128)(2,1)}, u32[]{:S(2)}) copy-start(bf16[128,1024]{0,1:T(8,128)(2,1)} %copy.118) | copy-start | bytes 786436
  180.4 9.2 %copy-start.22 = (bf16[128,1024]{0,1:T(8,128)(2,1)S(1)}, bf16[128,1024]{0,1:T(8,128)(2,1)}, u32[]{:S(2)}) copy-start(bf16[128,1024]{0,1:T(8,128)(2,1)} %copy.119) | copy-start | bytes 786436
  183.9 6.1 %copy-start.20 = (bf16[128,1024]{0,1:T(8,128)(2,1)S(1)}, bf16[128,1024]{0,1:T(8,128)(2,1)}, u32[]{:S(2)}) copy-start(bf16[128,1024]{0,1:T(8,128)(2,1)} %copy.120) | copy-start | bytes 786436
  191.3 1.9 copy-start.23
  191.3 2.2 %copy-start.21 = (bf16[128,1024]{0,1:T(8,128)(2,1)S(1)}, bf16[128,1024]{0,1:T(8,128)(2,1)}, u32[]{:S(2)}) copy-start(bf16[128,1024]{0,1:T(8,128)(2,1)} %copy.99) | copy-start | bytes 786436
  191.3 2.6 %copy-start.19 = (bf16[128,1024]{0,1:T(8,128)(2,1)S(1)}, bf16[128,1024]{0,1:T(8,128)(2,1)}, u32[]{:S(2)}) copy-start(bf16[128,1024]{0,1:T(8,128)(2,1)} %copy.100) | copy-start | bytes 786436
  192.3 2.2 %copy-start.17 = (bf16[128,1024]{0,1:T(8,128)(2,1)S(1)}, bf16[128,1024]{0,1:T(8,128)(2,1)}, u32[]{:S(2)}) copy-start(bf16[128,1024]{0,1:T(8,128)(2,1)} %copy.101) | copy-start | bytes 786436
  195.7 1.7 copy-start.8
  195.7 2.0 copy-start.6
  195.8 2.3 %copy-start.4 = (bf16[128,1024]{0,1:T(8,128)(2,1)S(1)}, bf16[128,1024]{0,1:T(8,128)(2,1)}, u32[]{:S(2)}) copy-start(bf16[128,1024]{0,1:T(8,128)(2,1)} %copy.128) | copy-start | bytes 786436
  196.8 1.5 copy-start.14
  196.8 1.8 copy-start.10
  196.8 2.1 %copy-start.9 = (bf16[128,1024]{0,1:T(8,128)(2,1)S(1)}, bf16[128,1024]{0,1:T(8,128)(2,1)}, u32[]{:S(2)}) copy-start(bf16[128,1024]{0,1:T(8,128)(2,1)} %copy.103) | copy-start | bytes 786436
  197.1 2.1 %copy-start.7 = (bf16[128,1024]{0,1:T(8,128)(2,1)S(1)}, bf16[128,1024]{0,1:T(8,128)(2,1)}, u32[]{:S(2)}) copy-start(bf16[128,1024]{0,1:T(8,128)(2,1)} %copy.105) | copy-start | bytes 786436
  197.4 2.1 %copy-start.5 = (bf16[128,1024]{0,1:T(8,128)(2,1)S(1)}, bf16[128,1024]{0,1:T(8,128)(2,1)}, u32[]{:S(2)}) copy-start(bf16[128,1024]{0,1:T(8,128)(2,1)} %copy.107) | copy-start | bytes 786436
  198.0 2.0 %copy-start.13 = (bf16[128,1024]{0,1:T(8,128)(2,1)S(1)}, bf16[128,1024]{0,1:T(8,128)(2,1)}, u32[]{:S(2)}) copy-start(bf16[128,1024]{0,1:T(8,128)(2,1)} %copy.111) | copy-start | bytes 786436
  198.3 2.0 %copy-start.3 = (bf16[1024,1024]{1,0:T(8,128)(2,1)S(1)}, bf16[1024,1024]{1,0:T(8,128)(2,1)}, u32[]{:S(2)}) copy-start(bf16[1024,1024]{1,0:T(8,128)(2,1)} %param.17) | copy-start | bytes 6291460
  198.3 2.0 %copy-start.15 = (bf16[256,1024]{1,0:T(8,128)(2,1)S(1)}, bf16[256,1024]{1,0:T(8,128)(2,1)}, u32[]{:S(2)}) copy-start(bf16[256,1024]{1,0:T(8,128)(2,1)} %param.12) | copy-start | bytes 1572868
  198.9 3.2 %copy-start.1 = (bf16[1024,1024]{1,0:T(8,128)(2,1)S(1)}, bf16[1024,1024]{1,0:T(8,128)(2,1)}, u32[]{:S(2)}) copy-start(bf16[1024,1024]{1,0:T(8,128)(2,1)} %param.11) | copy-start | bytes 6291460
  (5 other events, 6.2 us)
where the time goes:
time: 204 us; the launch traced here: 202 us
  between operations  74.6 us (37%)
  local copies, waits for them, and re-layouts  68 us (33%)
  other arithmetic  25.9 us (13%)
  matrix products  20 us (10%)
  starting transfers between devices  13.5 us (7%)
    slice x22, local copies, waits for them, and re-layouts, attend_one(): tile[:, model_width:].reshape(tile_rows, HEADS, head_size)  30.6 us
    slice x14, local copies, waits for them, and re-layouts, attend_one(): key_heads = tile[:, :model_width].reshape(tile_rows, HEADS, head_size)  16.6 us
    select_n x6, other arithmetic, pick_tile(): picked = jnp.where(source_index == number, other, picked)  15.3 us
    ppermute x8, starting transfers between devices, from_behind(): return lax.ppermute(block, axis, route)  13.5 us
    gather x4, local copies, waits for them, and re-layouts, per_device(): received.append(fetch(jnp.take(payload, requested, axis=0), offset))  12.2 us
    dot_general x1, matrix products, per_device(): jnp.dot(grid_latents, w_keyval, preferred_element_type=jnp.float32)  8.18 us
    select_n x6, other arithmetic, per_device(): received.append(fetch(jnp.take(payload, requested, axis=0), offset))  4.61 us
    dot_general x12, matrix products, attend_one(): jnp.einsum('qhd,khd->hqk', query_heads, key_heads, preferred_element_type...  4.38 us
  transfers between devices with their start and end apart: 8, of which 0 were waited for; matrix products, arithmetic and copies ran while one was open for 12% of the time, Pallas kernels for 0%

commit v1 on v0

v1 whole, which is shorter than its diff:
```python
import functools

import jax
import jax.numpy as jnp
from jax import lax
from jax.experimental import pallas as pl
from jax.experimental.pallas import tpu as pltpu
from jax.sharding import PartitionSpec as P

HEADS = 16
TILE = 128
REACH = 2
CAP = 2
GROUP = 4
VMEM_LIMIT = 56 * 1024 * 1024


def plan_requests(tiles, live, own_tiles, offsets, position, node_count):
    owner = tiles // own_tiles
    local = tiles % own_tiles
    away = (owner - position + node_count + REACH) % node_count - REACH
    ids = jnp.arange(own_tiles, dtype=jnp.int32)
    slot_ids = jnp.arange(CAP, dtype=jnp.int32)
    requests = []
    table = jnp.where(away == 0, local, 0)
    for number, offset in enumerate(offsets):
        wanted = (live > 0) & (away == offset)
        needed = jnp.any(wanted[:, :, None] & (local[:, :, None] == ids), axis=(0, 1))
        before = jnp.sum(
            jnp.where(needed[None, :] & (ids[None, :] < ids[:, None]), 1, 0), axis=1
        )
        chosen = needed[None, :] & (before[None, :] == slot_ids[:, None])
        requests.append(jnp.sum(jnp.where(chosen, ids[None, :], 0), axis=1))
        place = jnp.sum(jnp.where(needed & (ids < local[:, :, None]), 1, 0), axis=2)
        table = jnp.where(wanted, own_tiles + number * CAP + place, table)
    return requests, table


def pick_kernel(request_ref, grid_ref, *refs):
    outs, sems = refs[:-1], refs[-1]
    copies = []
    for number, out in enumerate(outs):
        for slot in range(CAP):
            tile = request_ref[number * CAP + slot]
            copies.append(
                pltpu.make_async_copy(
                    grid_ref.at[tile], out.at[slot], sems.at[number * CAP + slot]
                )
            )
    for copy in copies:
        copy.start()
    for copy in copies:
        copy.wait()


def pick(requested, grid):
    count = requested.shape[0] // CAP
    return pl.pallas_call(
        pick_kernel,
        out_shape=[jax.ShapeDtypeStruct((CAP,) + grid.shape[1:], grid.dtype)] * count,
        in_specs=[
            pl.BlockSpec(memory_space=pltpu.SMEM),
            pl.BlockSpec(memory_space=pl.ANY),
        ],
        out_specs=[pl.BlockSpec(memory_space=pl.ANY)] * count,
        scratch_shapes=[pltpu.SemaphoreType.DMA((count * CAP,))],
        name="pick",
    )(requested, grid)


def encode_kernel(
    count, table_ref, live_ref, own_ref, w_keyval_ref, query_ref, w_out_ref, mesh_ref, *refs
):
    received = refs[:count]
    out_ref, keyval, attended, own_sem = refs[count:]
    own_tiles = own_ref.shape[0]
    tile_rows = keyval.shape[1]
    width = query_ref.shape[1]
    head_size = width // HEADS
    span = GROUP * head_size
    slots = table_ref.shape[1]
    mesh_tiles = table_ref.shape[0]

    own_copy = pltpu.make_async_copy(own_ref, keyval.at[0:own_tiles], own_sem)
    own_copy.start()
    for number, tiles in enumerate(received):
        rows = tiles[...].reshape(CAP * tile_rows, width)
        for part in range(0, 2 * width, 512):
            columns = slice(part, part + 512)
            done = jnp.dot(rows, w_keyval_ref[:, columns], preferred_element_type=jnp.float32)
            first = own_tiles + number * CAP
            keyval[first : first + CAP, :, columns] = done.astype(keyval.dtype).reshape(
                CAP, tile_rows, 512
            )
    own_copy.wait()

    lane_head = lax.broadcasted_iota(jnp.int32, (1, span), 1) // head_size
    key_slot = lax.broadcasted_iota(jnp.int32, (1, slots * tile_rows), 1) // tile_rows
    for tile in range(mesh_tiles):
        rows = slice(tile * tile_rows, (tile + 1) * tile_rows)
        bias = jnp.zeros((1, slots * tile_rows), jnp.float32)
        for slot in range(slots):
            off = jnp.where(live_ref[tile, slot] > 0, 0.0, -1e30)
            bias = jnp.where(key_slot == slot, off, bias)
        index = [table_ref[tile, slot] for slot in range(slots)]
        for group in range(HEADS // GROUP):
            columns = slice(group * span, (group + 1) * span)
            behind = slice(width + group * span, width + (group + 1) * span)
            query = query_ref[rows, columns]
            stacked = jnp.concatenate(
                [jnp.where(lane_head == h, query, jnp.zeros_like(query)) for h in range(GROUP)],
                axis=0,
            )
            keys = jnp.concatenate([keyval[i, :, columns] for i in index], axis=0)
            values = jnp.concatenate([keyval[i, :, behind] for i in index], axis=0)
            scores = lax.dot_general(
                stacked, keys, (((1,), (1,)), ((), ())), preferred_element_type=jnp.float32
            )
            scores = scores + bias
            raised = jnp.exp(scores - jnp.max(scores, axis=-1, keepdims=True))
            share = 1.0 / jnp.sum(raised, axis=-1, keepdims=True)
            weights = (raised * share).astype(jnp.bfloat16)
            mixed = jnp.dot(weights, values, preferred_element_type=jnp.float32)
            total = jnp.zeros((tile_rows, span), jnp.float32)
            for h in range(GROUP):
                total = jnp.where(
                    lane_head == h, mixed[h * tile_rows : (h + 1) * tile_rows], total
                )
            attended[rows, columns] = total.astype(jnp.bfloat16)
    for part in range(0, width, 512):
        columns = slice(part, part + 512)
        out_ref[:, columns] = mesh_ref[:, columns].astype(jnp.float32) + jnp.dot(
            attended[...], w_out_ref[:, columns], preferred_element_type=jnp.float32
        )


def encode(table, live, own, w_keyval, query, w_out, mesh_latents, received):
    count = len(received)
    own_tiles, tile_rows, wide = own.shape
    vmem = pl.BlockSpec(memory_space=pltpu.VMEM)
    smem = pl.BlockSpec(memory_space=pltpu.SMEM)
    return pl.pallas_call(
        functools.partial(encode_kernel, count),
        out_shape=jax.ShapeDtypeStruct(mesh_latents.shape, jnp.float32),
        in_specs=[smem, smem, pl.BlockSpec(memory_space=pl.ANY)] + [vmem] * (4 + count),
        out_specs=vmem,
        scratch_shapes=[
            pltpu.VMEM((own_tiles + count * CAP, tile_rows, wide), jnp.bfloat16),
            pltpu.VMEM(mesh_latents.shape, jnp.bfloat16),
            pltpu.SemaphoreType.DMA,
        ],
        compiler_params=pltpu.CompilerParams(vmem_limit_bytes=VMEM_LIMIT),
        name="encode",
    )(table, live, own, w_keyval, query, w_out, mesh_latents, *received)


def per_device(
    grid_latents, mesh_latents, neighbour_tiles, neighbour_live, w_query, w_keyval, w_out
):
    width = w_query.shape[0]
    own_tiles = grid_latents.shape[0] // TILE
    node_count = lax.axis_size("nodes")
    position = lax.axis_index("nodes")
    offsets = [o for o in range(-REACH, REACH + 1) if o != 0]

    def route(shift):
        return [(i, (i + shift) % node_count) for i in range(node_count)]

    requests, table = plan_requests(
        neighbour_tiles, neighbour_live, own_tiles, offsets, position, node_count
    )
    asked = [lax.ppermute(r, "nodes", route(o)) for r, o in zip(requests, offsets)]
    picked = pick(jnp.concatenate(asked), grid_latents.reshape(own_tiles, TILE, width))
    received = [lax.ppermute(p, "nodes", route(-o)) for p, o in zip(picked, offsets)]
    own = jnp.dot(grid_latents, w_keyval, preferred_element_type=jnp.float32)
    own = own.astype(jnp.bfloat16).reshape(own_tiles, TILE, 2 * width)
    scale = (width // HEADS) ** -0.5
    query = jnp.dot(mesh_latents, w_query, preferred_element_type=jnp.float32) * scale
    query = query.astype(jnp.bfloat16)
    return encode(
        table, neighbour_live, own, w_keyval, query, w_out, mesh_latents, received
    )


def solution(mesh):
    return jax.shard_map(
        per_device,
        mesh=mesh,
        in_specs=(
            P(("groups", "nodes"), None),
            P(("groups", "nodes"), None),
            P("nodes", None),
            P("nodes", None),
            P(),
            P(),
            P(),
        ),
        out_specs=P(("groups", "nodes"), None),
        check_vma=False,
    )
```

time: 204 us -> 141 us (0.69)
  Pallas kernels: 0 us -> 80.3 us
  between operations: 74.6 us -> 0.27 us
  local copies, waits for them, and re-layouts: 68 us -> 1.71 us
  waiting for transfers between devices: 0.02 us -> 29.1 us
  other arithmetic: 25.9 us -> 4.38 us
  matrix products: 20 us -> 10.8 us
    pallas_call x0 -> x2, Pallas kernels: none -> 80.3 us  [the longest x1 65.4 us: pick(): pl.pallas_call(pick_kernel, out_shape=[jax.ShapeDtypeStruct((CAP,) + grid...]
    slice x42 -> x0, local copies, waits for them, and re-layouts: 52.6 us -> none  [the longest x22 30.6 us: attend_one(): tile[:, model_width:].reshape(tile_rows, HEADS, head_size)]
    ppermute x8, waiting for transfers between devices: 0.02 us -> 29.1 us  [the longest x4 29 us: per_device(): lax.ppermute(p, 'nodes', route(-o))]
    select_n x14 -> x2, other arithmetic: 20.8 us -> 1.44 us  [the longest x1 0.84 us: plan_requests(): local = tiles % own_tiles]
    gather x12 -> x0, local copies, waits for them, and re-layouts: 15.2 us -> none  [the longest x4 12.2 us: per_device(): received.append(fetch(jnp.take(payload, requested, axis=0), offset))]
    dot_general x27 -> x2, matrix products: 20 us -> 10.8 us  [the longest x1 9.25 us: per_device(): own = jnp.dot(grid_latents, w_keyval, preferred_element_type=jnp.float32)]
    convert_element_type x6 -> x0, other arithmetic: 2.06 us -> none  [the longest x2 2.05 us: attend_one(): weights = (raised / row_total).astype(jnp.bfloat16)]
  transfers between devices with their start and end apart: 8 -> 8, of which waited for: 0 -> 2; matrix products, arithmetic and copies ran while one was open for 12% -> 9% of each run, Pallas kernels for 0% -> 0%
where the time goes in v1:
time: 141 us
  Pallas kernels  80.3 us (57%)
  waiting for transfers between devices  29.1 us (21%)
  starting transfers between devices  14.5 us (10%)
  matrix products  10.8 us (8%)
  other arithmetic  4.38 us (3%)
  local copies, waits for them, and re-layouts  1.71 us (1%)
    pallas_call x1, Pallas kernels, pick(): pl.pallas_call(pick_kernel, out_shape=[jax.ShapeDtypeStruct((CAP,) + grid...  65.4 us
    ppermute x4, waiting for transfers between devices, per_device(): lax.ppermute(p, 'nodes', route(-o))  29 us
    pallas_call x1, Pallas kernels, encode(): pl.pallas_call(functools.partial(encode_kernel, count), out_shape=jax.Sha...  14.9 us
    dot_general x1, matrix products, per_device(): own = jnp.dot(grid_latents, w_keyval, preferred_element_type=jnp.float32)  9.25 us
    ppermute x4, starting transfers between devices, per_device(): lax.ppermute(r, 'nodes', route(o))  7.92 us
    ppermute x4, starting transfers between devices, per_device(): lax.ppermute(p, 'nodes', route(-o))  6.56 us
  transfers between devices with their start and end apart: 8, of which 2 were waited for; matrix products, arithmetic and copies ran while one was open for 9% of the time, Pallas kernels for 0%

profile of v1, /device:TPU:0, one launch (start us, length us, event | category | flops | bytes accessed | tf_op | source)
XLA Modules:
  0.0 140.9 jit_solution(1932767533013810099)
XLA Ops:
  0.0 0.8 and_select_fusion.8
  0.8 0.7 compare_and_fusion.2
  1.6 0.1 copy.12
  1.7 0.1 copy.15
  1.8 0.1 copy.18
  1.9 0.1 copy.8
  2.1 0.1 and_reduce_fusion.3
  2.2 0.1 select_reduce_fusion.1
  2.3 0.1 fusion.16
  2.5 0.5 collective-permute-start.2
  3.0 0.1 select_reduce_fusion.2
  3.1 0.1 fusion.15
  3.2 5.0 %collective-permute-start.1 = (s32[2]{0:T(128)S(1)}, s32[2]{0:T(128)S(1)}, u32[]{:S(2)}, u32[]{:S(2)}) collective-permute-start(s32[2]{0:T(128)S(1)} %fusion.15), channel_id=1, source_target_pairs={{0,15},{1,0},{2,1},{3,2},{4,3},{5,4},{6,5},{7,6},{8,7},{9,8},{10,9... | collective-permute-start | bytes 32 | tf_op jit(solution)/shard_map/ppermute | solution.py:172
  8.2 0.1 select_reduce_fusion.3
  8.3 0.1 fusion.14
  8.5 2.3 %collective-permute-start = (s32[2]{0:T(128)S(1)}, s32[2]{0:T(128)S(1)}, u32[]{:S(2)}, u32[]{:S(2)}) collective-permute-start(s32[2]{0:T(128)S(1)} %fusion.14), channel_id=1, source_target_pairs={{0,14},{1,15},{2,0},{3,1},{4,2},{5,3},{6,4},{7,5},{8,6},{9,7},{10,... | collective-permute-start | bytes 32 | tf_op jit(solution)/shard_map/ppermute | solution.py:172
  10.8 0.1 select_reduce_fusion
  10.9 0.1 fusion.17
  11.1 0.6 fusion.1
  11.7 0.1 copy.11
  11.7 0.1 copy.20
  12.0 9.2 %convolution_convert_fusion = bf16[1024,2048]{1,0:T(8,128)(2,1)} fusion(bf16[1024,1024]{1,0:T(8,128)(2,1)} %param.7, bf16[1024,2048]{1,0:T(8,128)(2,1)} %w_keyval_ref.1), kind=kOutput, calls=%fused_computation | convolution fusion | flops 4297064448 | bytes 10485760 | tf_op jit(solution)/shard_map/dot_general | solution.py:175
  21.3 0.6 pad_add_fusion.request_ref
  21.9 65.4 %pick.1 = (bf16[2,128,1024]{2,1,0:T(8,128)(2,1)}, bf16[2,128,1024]{2,1,0:T(8,128)(2,1)}, bf16[2,128,1024]{2,1,0:T(8,128)(2,1)}, bf16[2,128,1024]{2,1,0:T(8,128)(2,1)}) custom-call(s32[8]{0:T(128)} %pad_add_fusion.request_ref, bf16[8,128,1024]{2,1,0:T(8,128)(2,1)} %bitcast.7), custom_call_target="tpu_custom_call" | custom-call | tf_op jit(solution)/shard_map/pick/pallas_call | solution.py:58
  87.4 4.4 %collective-permute-start.6 = (bf16[2,128,1024]{2,1,0:T(8,128)(2,1)}, bf16[2,128,1024]{2,1,0:T(8,128)(2,1)S(1)}, u32[]{:S(2)}, u32[]{:S(2)}) collective-permute-start(bf16[2,128,1024]{2,1,0:T(8,128)(2,1)} %get-tuple-element.11), channel_id=1, source_target_pairs={{0,15},{1,0},{2,1},{3,2},{4,3},{5,4},{6,5},{7,6},{8,7},{9,8},{10,9... | collective-permute-start | bytes 1572872 | tf_op jit(solution)/shard_map/ppermute | solution.py:174
  91.8 2.0 %collective-permute-start.7 = (bf16[2,128,1024]{2,1,0:T(8,128)(2,1)}, bf16[2,128,1024]{2,1,0:T(8,128)(2,1)S(1)}, u32[]{:S(2)}, u32[]{:S(2)}) collective-permute-start(bf16[2,128,1024]{2,1,0:T(8,128)(2,1)} %get-tuple-element.12), channel_id=1, source_target_pairs={{0,14},{1,15},{2,0},{3,1},{4,2},{5,3},{6,4},{7,5},{8,6},{9,7},{10,... | collective-permute-start | bytes 1572872 | tf_op jit(solution)/shard_map/ppermute | solution.py:174
  93.9 0.6 fusion.13.table_ref
  94.5 1.5 %fusion.query_ref = bf16[256,1024]{1,0:T(8,128)(2,1)} fusion(bf16[256,1024]{1,0:T(8,128)(2,1)S(1)} %copy-done.1, bf16[1024,1024]{1,0:T(8,128)(2,1)S(1)} %copy-done), kind=kOutput, calls=%fused_computation.2 | convolution fusion | flops 537395200 | bytes 3145728 | tf_op jit(solution)/shard_map/dot_general | solution.py:178
  96.0 20.9 %collective-permute-done.4.refs_0_ = bf16[2,128,1024]{2,1,0:T(8,128)(2,1)S(1)} collective-permute-done((bf16[2,128,1024]{2,1,0:T(8,128)(2,1)}, bf16[2,128,1024]{2,1,0:T(8,128)(2,1)S(1)}, u32[]{:S(2)}, u32[]{:S(2)}) %collective-permute-start.4) | collective-permute-done | bytes 524320 | tf_op jit(solution)/shard_map/ppermute | solution.py:174
  116.9 8.1 %collective-permute-done.7.refs_3_ = bf16[2,128,1024]{2,1,0:T(8,128)(2,1)S(1)} collective-permute-done((bf16[2,128,1024]{2,1,0:T(8,128)(2,1)}, bf16[2,128,1024]{2,1,0:T(8,128)(2,1)S(1)}, u32[]{:S(2)}, u32[]{:S(2)}) %collective-permute-start.7) | collective-permute-done | bytes 524320 | tf_op jit(solution)/shard_map/ppermute | solution.py:174
  125.1 0.8 copy-done.5
  125.8 14.9 %encode.1 = f32[256,1024]{1,0:T(8,128)} custom-call(s32[2,6]{1,0:T(2,128)} %fusion.13.table_ref, s32[2,6]{1,0:T(2,128)} %live_ref.1, bf16[8,128,2048]{2,1,0:T(8,128)(2,1)} %bitcast.6, bf16[1024,2048]{1,0:T(8,128)(2,1)} %w_keyval_ref.1, bf16[256,1024]{1,0:T(8,128)(2,1)} %fusion.query_ref, bf16[1024,1024]{1,0:T(8,128)(2,1)} %w_out_ref.1, ...), custom_call_target="tpu_custom_call" | custom-call | tf_op jit(solution)/shard_map/encode/pallas_call | solution.py:142
  (26 shorter events, 0.5 us)
Async XLA Ops:
  0.0 94.5 %copy-start = (bf16[1024,1024]{1,0:T(8,128)(2,1)S(1)}, bf16[1024,1024]{1,0:T(8,128)(2,1)}, u32[]{:S(2)}) copy-start(bf16[1024,1024]{1,0:T(8,128)(2,1)} %param.11) | copy-start | bytes 6291460
  2.5 18.8 %collective-permute-start.2 = (s32[2]{0:T(128)S(1)}, s32[2]{0:T(128)S(1)}, u32[]{:S(2)}, u32[]{:S(2)}) collective-permute-start(s32[2]{0:T(128)S(1)} %fusion.16), channel_id=1, source_target_pairs={{0,1},{1,2},{2,3},{3,4},{4,5},{5,6},{6,7},{7,8},{8,9},{9,10},{10,1... | collective-permute-start | bytes 32 | tf_op jit(solution)/shard_map/ppermute | solution.py:172
  3.2 18.1 %collective-permute-start.1 = (s32[2]{0:T(128)S(1)}, s32[2]{0:T(128)S(1)}, u32[]{:S(2)}, u32[]{:S(2)}) collective-permute-start(s32[2]{0:T(128)S(1)} %fusion.15), channel_id=1, source_target_pairs={{0,15},{1,0},{2,1},{3,2},{4,3},{5,4},{6,5},{7,6},{8,7},{9,8},{10,9... | collective-permute-start | bytes 32 | tf_op jit(solution)/shard_map/ppermute | solution.py:172
  8.5 12.8 %collective-permute-start = (s32[2]{0:T(128)S(1)}, s32[2]{0:T(128)S(1)}, u32[]{:S(2)}, u32[]{:S(2)}) collective-permute-start(s32[2]{0:T(128)S(1)} %fusion.14), channel_id=1, source_target_pairs={{0,14},{1,15},{2,0},{3,1},{4,2},{5,3},{6,4},{7,5},{8,6},{9,7},{10,... | collective-permute-start | bytes 32 | tf_op jit(solution)/shard_map/ppermute | solution.py:172
  11.0 10.3 %collective-permute-start.3 = (s32[2]{0:T(128)S(1)}, s32[2]{0:T(128)S(1)}, u32[]{:S(2)}, u32[]{:S(2)}) collective-permute-start(s32[2]{0:T(128)S(1)} %fusion.17), channel_id=1, source_target_pairs={{0,2},{1,3},{2,4},{3,5},{4,6},{5,7},{6,8},{7,9},{8,10},{9,11},{10,... | collective-permute-start | bytes 32 | tf_op jit(solution)/shard_map/ppermute | solution.py:172
  21.3 72.6 %copy-start.6 = (s32[2,6]{1,0:T(2,128)S(1)}, s32[2,6]{1,0:T(2,128)}, u32[]{:S(2)}) copy-start(s32[2,6]{1,0:T(2,128)} %param.9) | copy-start | bytes 148
  21.3 73.2 %copy-start.1 = (bf16[256,1024]{1,0:T(8,128)(2,1)S(1)}, bf16[256,1024]{1,0:T(8,128)(2,1)}, u32[]{:S(2)}) copy-start(bf16[256,1024]{1,0:T(8,128)(2,1)} %mesh_ref.1) | copy-start | bytes 1572868
  87.3 29.6 %collective-permute-start.4 = (bf16[2,128,1024]{2,1,0:T(8,128)(2,1)}, bf16[2,128,1024]{2,1,0:T(8,128)(2,1)S(1)}, u32[]{:S(2)}, u32[]{:S(2)}) collective-permute-start(bf16[2,128,1024]{2,1,0:T(8,128)(2,1)} %get-tuple-element.9), channel_id=1, source_target_pairs={{0,2},{1,3},{2,4},{3,5},{4,6},{5,7},{6,8},{7,9},{8,10},{9,11},{10,... | collective-permute-start | bytes 1572872 | tf_op jit(solution)/shard_map/ppermute | solution.py:174
  87.4 29.5 %collective-permute-start.5 = (bf16[2,128,1024]{2,1,0:T(8,128)(2,1)}, bf16[2,128,1024]{2,1,0:T(8,128)(2,1)S(1)}, u32[]{:S(2)}, u32[]{:S(2)}) collective-permute-start(bf16[2,128,1024]{2,1,0:T(8,128)(2,1)} %get-tuple-element.10), channel_id=1, source_target_pairs={{0,1},{1,2},{2,3},{3,4},{4,5},{5,6},{6,7},{7,8},{8,9},{9,10},{10,1... | collective-permute-start | bytes 1572872 | tf_op jit(solution)/shard_map/ppermute | solution.py:174
  87.4 29.5 %collective-permute-start.6 = (bf16[2,128,1024]{2,1,0:T(8,128)(2,1)}, bf16[2,128,1024]{2,1,0:T(8,128)(2,1)S(1)}, u32[]{:S(2)}, u32[]{:S(2)}) collective-permute-start(bf16[2,128,1024]{2,1,0:T(8,128)(2,1)} %get-tuple-element.11), channel_id=1, source_target_pairs={{0,15},{1,0},{2,1},{3,2},{4,3},{5,4},{6,5},{7,6},{8,7},{9,8},{10,9... | collective-permute-start | bytes 1572872 | tf_op jit(solution)/shard_map/ppermute | solution.py:174
  91.8 33.2 %collective-permute-start.7 = (bf16[2,128,1024]{2,1,0:T(8,128)(2,1)}, bf16[2,128,1024]{2,1,0:T(8,128)(2,1)S(1)}, u32[]{:S(2)}, u32[]{:S(2)}) collective-permute-start(bf16[2,128,1024]{2,1,0:T(8,128)(2,1)} %get-tuple-element.12), channel_id=1, source_target_pairs={{0,14},{1,15},{2,0},{3,1},{4,2},{5,3},{6,4},{7,5},{8,6},{9,7},{10,... | collective-permute-start | bytes 1572872 | tf_op jit(solution)/shard_map/ppermute | solution.py:174
  116.9 8.2 %copy-start.2 = (bf16[2,128,1024]{2,1,0:T(8,128)(2,1)}, bf16[2,128,1024]{2,1,0:T(8,128)(2,1)S(1)}, u32[]{:S(2)}) copy-start(bf16[2,128,1024]{2,1,0:T(8,128)(2,1)S(1)} %collective-permute-done.4.refs_0_) | copy-start | bytes 1572868
  116.9 8.2 %copy-start.3 = (bf16[2,128,1024]{2,1,0:T(8,128)(2,1)}, bf16[2,128,1024]{2,1,0:T(8,128)(2,1)S(1)}, u32[]{:S(2)}) copy-start(bf16[2,128,1024]{2,1,0:T(8,128)(2,1)S(1)} %collective-permute-done.5.refs_1_) | copy-start | bytes 1572868
  116.9 8.1 %copy-start.4 = (bf16[2,128,1024]{2,1,0:T(8,128)(2,1)}, bf16[2,128,1024]{2,1,0:T(8,128)(2,1)S(1)}, u32[]{:S(2)}) copy-start(bf16[2,128,1024]{2,1,0:T(8,128)(2,1)S(1)} %collective-permute-done.6.refs_2_) | copy-start | bytes 1572868
  125.0 0.8 copy-start.5

commit v2 on v1

--- a/solution.py
+++ b/solution.py
@@ -62,7 +62,7 @@
             pl.BlockSpec(memory_space=pltpu.SMEM),
             pl.BlockSpec(memory_space=pl.ANY),
         ],
-        out_specs=[pl.BlockSpec(memory_space=pl.ANY)] * count,
+        out_specs=[pl.BlockSpec(memory_space=pltpu.VMEM)] * count,
         scratch_shapes=[pltpu.SemaphoreType.DMA((count * CAP,))],
         name="pick",
     )(requested, grid)
@@ -172,6 +172,9 @@
     asked = [lax.ppermute(r, "nodes", route(o)) for r, o in zip(requests, offsets)]
     picked = pick(jnp.concatenate(asked), grid_latents.reshape(own_tiles, TILE, width))
     received = [lax.ppermute(p, "nodes", route(-o)) for p, o in zip(picked, offsets)]
+    grid_latents, mesh_latents, _ = lax.optimization_barrier(
+        (grid_latents, mesh_latents, picked)
+    )
     own = jnp.dot(grid_latents, w_keyval, preferred_element_type=jnp.float32)
     own = own.astype(jnp.bfloat16).reshape(own_tiles, TILE, 2 * width)
     scale = (width // HEADS) ** -0.5

time: 141 us -> 73.2 us (0.52)
  Pallas kernels: 80.3 us -> 19 us
  waiting for transfers between devices: 29.1 us -> 21.8 us
    pallas_call x1, Pallas kernels: 65.4 us -> 4.09 us  [pick(): pl.pallas_call(pick_kernel, out_shape=[jax.ShapeDtypeStruct((CAP,) + grid...]
    ppermute x4, waiting for transfers between devices: 29 us -> 17.8 us  [per_device(): lax.ppermute(p, 'nodes', route(-o))]
    ppermute x4, waiting for transfers between devices: 0.01 us -> 4.01 us  [per_device(): lax.ppermute(r, 'nodes', route(o))]
  transfers between devices with their start and end apart: 8 -> 8, of which waited for: 2 -> 3; matrix products, arithmetic and copies ran while one was open for 9% -> 19% of each run, Pallas kernels for 0% -> 0%
where the time goes in v2:
time: 73.2 us; the launch traced here: 72.9 us
  waiting for transfers between devices  21.8 us (30%)
  Pallas kernels  19 us (26%)
  starting transfers between devices  14.4 us (20%)
  matrix products  10.8 us (15%)
  other arithmetic  5.13 us (7%)
  local copies, waits for them, and re-layouts  1.71 us (2%)
    ppermute x4, waiting for transfers between devices, per_device(): lax.ppermute(p, 'nodes', route(-o))  17.8 us
    pallas_call x1, Pallas kernels, encode(): pl.pallas_call(functools.partial(encode_kernel, count), out_shape=jax.Sha...  14.9 us
    dot_general x1, matrix products, per_device(): own = jnp.dot(grid_latents, w_keyval, preferred_element_type=jnp.float32)  9.25 us
    ppermute x4, starting transfers between devices, per_device(): lax.ppermute(r, 'nodes', route(o))  7.92 us
    ppermute x4, starting transfers between devices, per_device(): lax.ppermute(p, 'nodes', route(-o))  6.51 us
    pallas_call x1, Pallas kernels, pick(): pl.pallas_call(pick_kernel, out_shape=[jax.ShapeDtypeStruct((CAP,) + grid...  4.09 us
    ppermute x4, waiting for transfers between devices, per_device(): lax.ppermute(r, 'nodes', route(o))  4.01 us
    dot_general x1, matrix products, per_device(): jnp.dot(mesh_latents, w_query, preferred_element_type=jnp.float32) * scale  1.51 us
  transfers between devices with their start and end apart: 8, of which 3 were waited for; matrix products, arithmetic and copies ran while one was open for 19% of the time, Pallas kernels for 0%

profile of v2, /device:TPU:0, one launch (start us, length us, event | category | flops | bytes accessed | tf_op | source)
XLA Modules:
  0.0 72.9 jit_solution(1056760946720385335)
XLA Ops:
  0.0 0.8 %and_select_fusion.8 = s32[2,6]{1,0:T(2,128)S(1)} fusion(s32[2,6]{1,0:T(2,128)} %param.9), kind=kLoop, calls=%fused_computation.36 | loop fusion | flops 132 | bytes 96 | tf_op jit(solution)/shard_map/jit(remainder)/select_n | solution.py:20
  0.8 0.7 compare_and_fusion.2
  1.6 0.1 copy.12
  1.7 0.1 copy.15
  1.8 0.1 copy.18
  1.9 0.1 copy.8
  2.1 0.1 and_reduce_fusion.3
  2.2 0.1 select_reduce_fusion.1
  2.3 0.1 fusion.16
  2.5 0.5 collective-permute-start.2
  3.0 0.1 select_reduce_fusion.2
  3.1 0.1 fusion.15
  3.2 5.0 %collective-permute-start.1 = (s32[2]{0:T(128)S(1)}, s32[2]{0:T(128)S(1)}, u32[]{:S(2)}, u32[]{:S(2)}) collective-permute-start(s32[2]{0:T(128)S(1)} %fusion.15), channel_id=1, source_target_pairs={{0,15},{1,0},{2,1},{3,2},{4,3},{5,4},{6,5},{7,6},{8,7},{9,8},{10,9... | collective-permute-start | bytes 32 | tf_op jit(solution)/shard_map/ppermute | solution.py:172
  8.2 0.1 select_reduce_fusion.3
  8.3 0.1 fusion.14
  8.5 2.3 %collective-permute-start = (s32[2]{0:T(128)S(1)}, s32[2]{0:T(128)S(1)}, u32[]{:S(2)}, u32[]{:S(2)}) collective-permute-start(s32[2]{0:T(128)S(1)} %fusion.14), channel_id=1, source_target_pairs={{0,14},{1,15},{2,0},{3,1},{4,2},{5,3},{6,4},{7,5},{8,6},{9,7},{10,... | collective-permute-start | bytes 32 | tf_op jit(solution)/shard_map/ppermute | solution.py:172
  10.8 0.1 select_reduce_fusion
  10.9 0.1 fusion.17
  11.1 0.6 fusion.1
  11.7 0.1 copy.11
  12.0 1.3 %fusion.13.table_ref = s32[2,6]{1,0:T(2,128)} fusion(s32[2,6]{1,0:T(2,128)S(1)} %get-tuple-element.27, s32[2,6]{1,0:T(2,128)S(1)} %copy.20, s32[2,6]{1,0:T(2,128)S(1)} %copy.17, s32[2,6]{1,0:T(2,128)S(1)} %copy.14, s32[2,6]{1,0:T(2,128)S(1)} %copy.11, pred[2,6]{1,0:T(4,128)(4,1)S(1)} %get-tuple-element.26, s32[2,6]{1,0:T(2,128)} %param.9), kind=kLoop, calls=%fused_computation.47 | loop fusion | flops 348 | bytes 348 | tf_op jit(solution)/shard_map/jit(_where)/select_n | solution.py:35
  13.3 4.0 %collective-permute-done.3 = s32[2]{0:T(128)S(1)} collective-permute-done((s32[2]{0:T(128)S(1)}, s32[2]{0:T(128)S(1)}, u32[]{:S(2)}, u32[]{:S(2)}) %collective-permute-start.3) | collective-permute-done | bytes 40 | tf_op jit(solution)/shard_map/ppermute | solution.py:172
  17.3 0.7 pad_add_fusion.request_ref
  18.0 4.1 %pick.1 = (bf16[2,128,1024]{2,1,0:T(8,128)(2,1)}, bf16[2,128,1024]{2,1,0:T(8,128)(2,1)}, bf16[2,128,1024]{2,1,0:T(8,128)(2,1)}, bf16[2,128,1024]{2,1,0:T(8,128)(2,1)}) custom-call(s32[8]{0:T(128)} %pad_add_fusion.request_ref, bf16[8,128,1024]{2,1,0:T(8,128)(2,1)} %bitcast.7), custom_call_target="tpu_custom_call" | custom-call | tf_op jit(solution)/shard_map/pick/pallas_call | solution.py:58
  22.2 4.4 %collective-permute-start.6 = (bf16[2,128,1024]{2,1,0:T(8,128)(2,1)}, bf16[2,128,1024]{2,1,0:T(8,128)(2,1)S(1)}, u32[]{:S(2)}, u32[]{:S(2)}) collective-permute-start(bf16[2,128,1024]{2,1,0:T(8,128)(2,1)} %get-tuple-element.13), channel_id=1, source_target_pairs={{0,15},{1,0},{2,1},{3,2},{4,3},{5,4},{6,5},{7,6},{8,7},{9,8},{10,9... | collective-permute-start | bytes 1572872 | tf_op jit(solution)/shard_map/ppermute | solution.py:174
  26.7 2.0 %collective-permute-start.7 = (bf16[2,128,1024]{2,1,0:T(8,128)(2,1)}, bf16[2,128,1024]{2,1,0:T(8,128)(2,1)S(1)}, u32[]{:S(2)}, u32[]{:S(2)}) collective-permute-start(bf16[2,128,1024]{2,1,0:T(8,128)(2,1)} %get-tuple-element.14), channel_id=1, source_target_pairs={{0,14},{1,15},{2,0},{3,1},{4,2},{5,3},{6,4},{7,5},{8,6},{9,7},{10,... | collective-permute-start | bytes 1572872 | tf_op jit(solution)/shard_map/ppermute | solution.py:174
  28.6 9.2 %convolution_convert_fusion = bf16[1024,2048]{1,0:T(8,128)(2,1)} fusion(bf16[1024,1024]{1,0:T(8,128)(2,1)} %param.7, bf16[1024,2048]{1,0:T(8,128)(2,1)} %w_keyval_ref.1), kind=kOutput, calls=%fused_computation | convolution fusion | flops 4297064448 | bytes 10485760 | tf_op jit(solution)/shard_map/dot_general | solution.py:178
  37.9 1.5 %fusion.query_ref = bf16[256,1024]{1,0:T(8,128)(2,1)} fusion(bf16[256,1024]{1,0:T(8,128)(2,1)S(1)} %copy-done.1, bf16[1024,1024]{1,0:T(8,128)(2,1)S(1)} %copy-done), kind=kOutput, calls=%fused_computation.2 | convolution fusion | flops 537395200 | bytes 3145728 | tf_op jit(solution)/shard_map/dot_general | solution.py:181
  39.4 11.2 %collective-permute-done.4.refs_0_ = bf16[2,128,1024]{2,1,0:T(8,128)(2,1)S(1)} collective-permute-done((bf16[2,128,1024]{2,1,0:T(8,128)(2,1)}, bf16[2,128,1024]{2,1,0:T(8,128)(2,1)S(1)}, u32[]{:S(2)}, u32[]{:S(2)}) %collective-permute-start.4) | collective-permute-done | bytes 524320 | tf_op jit(solution)/shard_map/ppermute | solution.py:174
  50.6 6.6 %collective-permute-done.7.refs_3_ = bf16[2,128,1024]{2,1,0:T(8,128)(2,1)S(1)} collective-permute-done((bf16[2,128,1024]{2,1,0:T(8,128)(2,1)}, bf16[2,128,1024]{2,1,0:T(8,128)(2,1)S(1)}, u32[]{:S(2)}, u32[]{:S(2)}) %collective-permute-start.7) | collective-permute-done | bytes 524320 | tf_op jit(solution)/shard_map/ppermute | solution.py:174
  57.2 0.8 %copy-done.5 = bf16[2,128,1024]{2,1,0:T(8,128)(2,1)} copy-done((bf16[2,128,1024]{2,1,0:T(8,128)(2,1)}, bf16[2,128,1024]{2,1,0:T(8,128)(2,1)S(1)}, u32[]{:S(2)}) %copy-start.5) | copy-done | bytes 524312
  58.0 14.9 %encode.1 = f32[256,1024]{1,0:T(8,128)} custom-call(s32[2,6]{1,0:T(2,128)} %fusion.13.table_ref, s32[2,6]{1,0:T(2,128)} %live_ref.1, bf16[8,128,2048]{2,1,0:T(8,128)(2,1)} %bitcast.6, bf16[1024,2048]{1,0:T(8,128)(2,1)} %w_keyval_ref.1, bf16[256,1024]{1,0:T(8,128)(2,1)} %fusion.query_ref, bf16[1024,1024]{1,0:T(8,128)(2,1)} %w_out_ref.1, ...), custom_call_target="tpu_custom_call" | custom-call | tf_op jit(solution)/shard_map/encode/pallas_call | solution.py:142
  (24 shorter events, 0.6 us)
Async XLA Ops:
  0.0 37.9 %copy-start = (bf16[1024,1024]{1,0:T(8,128)(2,1)S(1)}, bf16[1024,1024]{1,0:T(8,128)(2,1)}, u32[]{:S(2)}) copy-start(bf16[1024,1024]{1,0:T(8,128)(2,1)} %param.11) | copy-start | bytes 6291460
  2.5 10.9 %collective-permute-start.2 = (s32[2]{0:T(128)S(1)}, s32[2]{0:T(128)S(1)}, u32[]{:S(2)}, u32[]{:S(2)}) collective-permute-start(s32[2]{0:T(128)S(1)} %fusion.16), channel_id=1, source_target_pairs={{0,1},{1,2},{2,3},{3,4},{4,5},{5,6},{6,7},{7,8},{8,9},{9,10},{10,1... | collective-permute-start | bytes 32 | tf_op jit(solution)/shard_map/ppermute | solution.py:172
  3.2 10.1 %collective-permute-start.1 = (s32[2]{0:T(128)S(1)}, s32[2]{0:T(128)S(1)}, u32[]{:S(2)}, u32[]{:S(2)}) collective-permute-start(s32[2]{0:T(128)S(1)} %fusion.15), channel_id=1, source_target_pairs={{0,15},{1,0},{2,1},{3,2},{4,3},{5,4},{6,5},{7,6},{8,7},{9,8},{10,9... | collective-permute-start | bytes 32 | tf_op jit(solution)/shard_map/ppermute | solution.py:172
  8.5 4.9 %collective-permute-start = (s32[2]{0:T(128)S(1)}, s32[2]{0:T(128)S(1)}, u32[]{:S(2)}, u32[]{:S(2)}) collective-permute-start(s32[2]{0:T(128)S(1)} %fusion.14), channel_id=1, source_target_pairs={{0,14},{1,15},{2,0},{3,1},{4,2},{5,3},{6,4},{7,5},{8,6},{9,7},{10,... | collective-permute-start | bytes 32 | tf_op jit(solution)/shard_map/ppermute | solution.py:172
  11.0 6.3 %collective-permute-start.3 = (s32[2]{0:T(128)S(1)}, s32[2]{0:T(128)S(1)}, u32[]{:S(2)}, u32[]{:S(2)}) collective-permute-start(s32[2]{0:T(128)S(1)} %fusion.17), channel_id=1, source_target_pairs={{0,2},{1,3},{2,4},{3,5},{4,6},{5,7},{6,8},{7,9},{8,10},{9,11},{10,... | collective-permute-start | bytes 32 | tf_op jit(solution)/shard_map/ppermute | solution.py:172
  22.1 28.5 %collective-permute-start.4 = (bf16[2,128,1024]{2,1,0:T(8,128)(2,1)}, bf16[2,128,1024]{2,1,0:T(8,128)(2,1)S(1)}, u32[]{:S(2)}, u32[]{:S(2)}) collective-permute-start(bf16[2,128,1024]{2,1,0:T(8,128)(2,1)} %get-tuple-element.11), channel_id=1, source_target_pairs={{0,2},{1,3},{2,4},{3,5},{4,6},{5,7},{6,8},{7,9},{8,10},{9,11},{10,... | collective-permute-start | bytes 1572872 | tf_op jit(solution)/shard_map/ppermute | solution.py:174
  22.2 28.5 %collective-permute-start.5 = (bf16[2,128,1024]{2,1,0:T(8,128)(2,1)}, bf16[2,128,1024]{2,1,0:T(8,128)(2,1)S(1)}, u32[]{:S(2)}, u32[]{:S(2)}) collective-permute-start(bf16[2,128,1024]{2,1,0:T(8,128)(2,1)} %get-tuple-element.12), channel_id=1, source_target_pairs={{0,1},{1,2},{2,3},{3,4},{4,5},{5,6},{6,7},{7,8},{8,9},{9,10},{10,1... | collective-permute-start | bytes 1572872 | tf_op jit(solution)/shard_map/ppermute | solution.py:174
  22.2 28.4 %collective-permute-start.6 = (bf16[2,128,1024]{2,1,0:T(8,128)(2,1)}, bf16[2,128,1024]{2,1,0:T(8,128)(2,1)S(1)}, u32[]{:S(2)}, u32[]{:S(2)}) collective-permute-start(bf16[2,128,1024]{2,1,0:T(8,128)(2,1)} %get-tuple-element.13), channel_id=1, source_target_pairs={{0,15},{1,0},{2,1},{3,2},{4,3},{5,4},{6,5},{7,6},{8,7},{9,8},{10,9... | collective-permute-start | bytes 1572872 | tf_op jit(solution)/shard_map/ppermute | solution.py:174
  26.6 11.2 %copy-start.1 = (bf16[256,1024]{1,0:T(8,128)(2,1)S(1)}, bf16[256,1024]{1,0:T(8,128)(2,1)}, u32[]{:S(2)}) copy-start(bf16[256,1024]{1,0:T(8,128)(2,1)} %mesh_ref) | copy-start | bytes 1572868
  26.7 30.6 %collective-permute-start.7 = (bf16[2,128,1024]{2,1,0:T(8,128)(2,1)}, bf16[2,128,1024]{2,1,0:T(8,128)(2,1)S(1)}, u32[]{:S(2)}, u32[]{:S(2)}) collective-permute-start(bf16[2,128,1024]{2,1,0:T(8,128)(2,1)} %get-tuple-element.14), channel_id=1, source_target_pairs={{0,14},{1,15},{2,0},{3,1},{4,2},{5,3},{6,4},{7,5},{8,6},{9,7},{10,... | collective-permute-start | bytes 1572872 | tf_op jit(solution)/shard_map/ppermute | solution.py:174
  50.6 6.6 %copy-start.2 = (bf16[2,128,1024]{2,1,0:T(8,128)(2,1)}, bf16[2,128,1024]{2,1,0:T(8,128)(2,1)S(1)}, u32[]{:S(2)}) copy-start(bf16[2,128,1024]{2,1,0:T(8,128)(2,1)S(1)} %collective-permute-done.4.refs_0_) | copy-start | bytes 1572868
  50.6 6.6 %copy-start.3 = (bf16[2,128,1024]{2,1,0:T(8,128)(2,1)}, bf16[2,128,1024]{2,1,0:T(8,128)(2,1)S(1)}, u32[]{:S(2)}) copy-start(bf16[2,128,1024]{2,1,0:T(8,128)(2,1)S(1)} %collective-permute-done.5.refs_1_) | copy-start | bytes 1572868
  50.6 6.6 %copy-start.4 = (bf16[2,128,1024]{2,1,0:T(8,128)(2,1)}, bf16[2,128,1024]{2,1,0:T(8,128)(2,1)S(1)}, u32[]{:S(2)}) copy-start(bf16[2,128,1024]{2,1,0:T(8,128)(2,1)S(1)} %collective-permute-done.6.refs_2_) | copy-start | bytes 1572868
  57.2 0.8 %copy-start.5 = (bf16[2,128,1024]{2,1,0:T(8,128)(2,1)}, bf16[2,128,1024]{2,1,0:T(8,128)(2,1)S(1)}, u32[]{:S(2)}) copy-start(bf16[2,128,1024]{2,1,0:T(8,128)(2,1)S(1)} %collective-permute-done.7.refs_3_) | copy-start | bytes 1572868

commit v3 on v1

--- a/solution.py
+++ b/solution.py
@@ -12,7 +12,8 @@
 REACH = 2
 CAP = 2
 GROUP = 4
-VMEM_LIMIT = 56 * 1024 * 1024
+CHUNK = 256
+VMEM_LIMIT = 44 * 1024 * 1024
 
 
 def plan_requests(tiles, live, own_tiles, offsets, position, node_count):
@@ -36,63 +37,118 @@
     return requests, table
 
 
-def pick_kernel(request_ref, grid_ref, *refs):
-    outs, sems = refs[:-1], refs[-1]
-    copies = []
-    for number, out in enumerate(outs):
-        for slot in range(CAP):
-            tile = request_ref[number * CAP + slot]
-            copies.append(
-                pltpu.make_async_copy(
-                    grid_ref.at[tile], out.at[slot], sems.at[number * CAP + slot]
-                )
-            )
-    for copy in copies:
-        copy.start()
-    for copy in copies:
-        copy.wait()
-
-
-def pick(requested, grid):
-    count = requested.shape[0] // CAP
-    return pl.pallas_call(
-        pick_kernel,
-        out_shape=[jax.ShapeDtypeStruct((CAP,) + grid.shape[1:], grid.dtype)] * count,
-        in_specs=[
-            pl.BlockSpec(memory_space=pltpu.SMEM),
-            pl.BlockSpec(memory_space=pl.ANY),
-        ],
-        out_specs=[pl.BlockSpec(memory_space=pl.ANY)] * count,
-        scratch_shapes=[pltpu.SemaphoreType.DMA((count * CAP,))],
-        name="pick",
-    )(requested, grid)
+def shifted(offset):
+    count = lax.axis_size("nodes")
+    return lax.rem(lax.axis_index("nodes") + (offset + count), count)
+
+
+def project(rows, weight_ref, store):
+    @pl.loop(0, weight_ref.shape[1] // CHUNK)
+    def _(step):
+        columns = pl.ds(pl.multiple_of(step * CHUNK, CHUNK), CHUNK)
+        store(
+            columns,
+            jnp.dot(rows(), weight_ref[:, columns], preferred_element_type=jnp.float32),
+        )
 
 
 def encode_kernel(
-    count, table_ref, live_ref, own_ref, w_keyval_ref, query_ref, w_out_ref, mesh_ref, *refs
+    offsets,
+    request_ref,
+    table_ref,
+    live_ref,
+    grid_ref,
+    mesh_ref,
+    w_query_hbm,
+    w_keyval_hbm,
+    w_out_hbm,
+    out_ref,
+    keyval,
+    query_ref,
+    attended,
+    sending,
+    received,
+    w_query_ref,
+    w_keyval_ref,
+    w_out_ref,
+    weight_sems,
+    send_sems,
+    recv_sems,
 ):
-    received = refs[:count]
-    out_ref, keyval, attended, own_sem = refs[count:]
-    own_tiles = own_ref.shape[0]
-    tile_rows = keyval.shape[1]
-    width = query_ref.shape[1]
+    own_tiles, tile_rows, width = grid_ref.shape
     head_size = width // HEADS
     span = GROUP * head_size
-    slots = table_ref.shape[1]
-    mesh_tiles = table_ref.shape[0]
-
-    own_copy = pltpu.make_async_copy(own_ref, keyval.at[0:own_tiles], own_sem)
-    own_copy.start()
-    for number, tiles in enumerate(received):
-        rows = tiles[...].reshape(CAP * tile_rows, width)
-        for part in range(0, 2 * width, 512):
-            columns = slice(part, part + 512)
-            done = jnp.dot(rows, w_keyval_ref[:, columns], preferred_element_type=jnp.float32)
-            first = own_tiles + number * CAP
-            keyval[first : first + CAP, :, columns] = done.astype(keyval.dtype).reshape(
-                CAP, tile_rows, 512
-            )
-    own_copy.wait()
+    mesh_tiles, slots = table_ref.shape
+
+    loads = [
+        pltpu.make_async_copy(source, target, weight_sems.at[number])
+        for number, (source, target) in enumerate(
+            (
+                (w_keyval_hbm, w_keyval_ref),
+                (w_query_hbm, w_query_ref),
+                (w_out_hbm, w_out_ref),
+            )
+        )
+    ]
+    for load in loads:
+        load.start()
+
+    barrier = pltpu.get_barrier_semaphore()
+    for offset in offsets:
+        pl.semaphore_signal(
+            barrier,
+            inc=1,
+            device_id={"nodes": shifted(offset)},
+            device_id_type=pl.DeviceIdType.MESH,
+        )
+    pl.semaphore_wait(barrier, len(offsets))
+
+    copies = []
+    for number, offset in enumerate(offsets):
+        for slot in range(CAP):
+            sending[number, slot] = grid_ref[request_ref[number * CAP + slot]]
+        copy = pltpu.make_async_remote_copy(
+            src_ref=sending.at[number],
+            dst_ref=received.at[number],
+            send_sem=send_sems.at[number],
+            recv_sem=recv_sems.at[number],
+            device_id={"nodes": shifted(-offset)},
+            device_id_type=pl.DeviceIdType.MESH,
+        )
+        copy.start()
+        copies.append(copy)
+
+    def keep(first, count):
+        def store(columns, done):
+            keyval[first : first + count, :, columns] = done.astype(keyval.dtype).reshape(
+                count, tile_rows, CHUNK
+            )
+
+        return store
+
+    loads[0].wait()
+    project(
+        lambda: grid_ref[...].reshape(own_tiles * tile_rows, width),
+        w_keyval_ref,
+        keep(0, own_tiles),
+    )
+    loads[1].wait()
+
+    def store_query(columns, done):
+        query_ref[:, columns] = (done * head_size ** (-0.5)).astype(query_ref.dtype)
+
+    project(lambda: mesh_ref[...], w_query_ref, store_query)
+    loads[2].wait()
+
+    pair = 2
+    for first in range(0, len(offsets), pair):
+        for copy in copies[first : first + pair]:
+            copy.wait()
+        project(
+            lambda: received[first : first + pair].reshape(pair * CAP * tile_rows, width),
+            w_keyval_ref,
+            keep(own_tiles + first * CAP, pair * CAP),
+        )
 
     lane_head = lax.broadcasted_iota(jnp.int32, (1, span), 1) // head_size
     key_slot = lax.broadcasted_iota(jnp.int32, (1, slots * tile_rows), 1) // tile_rows
@@ -134,24 +190,36 @@
         )
 
 
-def encode(table, live, own, w_keyval, query, w_out, mesh_latents, received):
-    count = len(received)
-    own_tiles, tile_rows, wide = own.shape
+def encode(offsets, request, table, live, grid, mesh_latents, w_query, w_keyval, w_out):
+    own_tiles, tile_rows, width = grid.shape
+    count = len(offsets)
     vmem = pl.BlockSpec(memory_space=pltpu.VMEM)
     smem = pl.BlockSpec(memory_space=pltpu.SMEM)
+    hbm = pl.BlockSpec(memory_space=pl.ANY)
+    bf16 = jnp.bfloat16
     return pl.pallas_call(
-        functools.partial(encode_kernel, count),
+        functools.partial(encode_kernel, offsets),
         out_shape=jax.ShapeDtypeStruct(mesh_latents.shape, jnp.float32),
-        in_specs=[smem, smem, pl.BlockSpec(memory_space=pl.ANY)] + [vmem] * (4 + count),
+        in_specs=[smem, smem, smem, vmem, vmem, hbm, hbm, hbm],
         out_specs=vmem,
         scratch_shapes=[
-            pltpu.VMEM((own_tiles + count * CAP, tile_rows, wide), jnp.bfloat16),
-            pltpu.VMEM(mesh_latents.shape, jnp.bfloat16),
-            pltpu.SemaphoreType.DMA,
+            pltpu.VMEM((own_tiles + count * CAP, tile_rows, 2 * width), bf16),
+            pltpu.VMEM(mesh_latents.shape, bf16),
+            pltpu.VMEM(mesh_latents.shape, bf16),
+            pltpu.VMEM((count, CAP, tile_rows, width), bf16),
+            pltpu.VMEM((count, CAP, tile_rows, width), bf16),
+            pltpu.VMEM(w_query.shape, bf16),
+            pltpu.VMEM(w_keyval.shape, bf16),
+            pltpu.VMEM(w_out.shape, bf16),
+            pltpu.SemaphoreType.DMA((3,)),
+            pltpu.SemaphoreType.DMA((count,)),
+            pltpu.SemaphoreType.DMA((count,)),
         ],
-        compiler_params=pltpu.CompilerParams(vmem_limit_bytes=VMEM_LIMIT),
+        compiler_params=pltpu.CompilerParams(
+            vmem_limit_bytes=VMEM_LIMIT, collective_id=0, has_side_effects=True
+        ),
         name="encode",
-    )(table, live, own, w_keyval, query, w_out, mesh_latents, *received)
+    )(request, table, live, grid, mesh_latents, w_query, w_keyval, w_out)
 
 
 def per_device(
@@ -161,7 +229,7 @@
     own_tiles = grid_latents.shape[0] // TILE
     node_count = lax.axis_size("nodes")
     position = lax.axis_index("nodes")
-    offsets = [o for o in range(-REACH, REACH + 1) if o != 0]
+    offsets = [sign * o for o in range(1, REACH + 1) for sign in (-1, 1)]
 
     def route(shift):
         return [(i, (i + shift) % node_count) for i in range(node_count)]
@@ -170,15 +238,16 @@
         neighbour_tiles, neighbour_live, own_tiles, offsets, position, node_count
     )
     asked = [lax.ppermute(r, "nodes", route(o)) for r, o in zip(requests, offsets)]
-    picked = pick(jnp.concatenate(asked), grid_latents.reshape(own_tiles, TILE, width))
-    received = [lax.ppermute(p, "nodes", route(-o)) for p, o in zip(picked, offsets)]
-    own = jnp.dot(grid_latents, w_keyval, preferred_element_type=jnp.float32)
-    own = own.astype(jnp.bfloat16).reshape(own_tiles, TILE, 2 * width)
-    scale = (width // HEADS) ** -0.5
-    query = jnp.dot(mesh_latents, w_query, preferred_element_type=jnp.float32) * scale
-    query = query.astype(jnp.bfloat16)
     return encode(
-        table, neighbour_live, own, w_keyval, query, w_out, mesh_latents, received
+        offsets,
+        jnp.concatenate(asked),
+        table,
+        neighbour_live,
+        grid_latents.reshape(own_tiles, TILE, width),
+        mesh_latents,
+        w_query,
+        w_keyval,
+        w_out,
     )
 
 

time: 141 us -> 68.3 us (0.48)
  Pallas kernels: 80.3 us -> 45.3 us
  waiting for transfers between devices: 29.1 us -> 0.72 us
  matrix products: 10.8 us -> 0 us
  local copies, waits for them, and re-layouts: 1.71 us -> 8.36 us
  starting transfers between devices: 14.5 us -> 9.77 us
    pallas_call x2 -> x1, Pallas kernels: 80.3 us -> 45.3 us  [encode(): pl.pallas_call(functools.partial(encode_kernel, offsets), out_shape=jax.S...]
    ppermute x4 -> x0, waiting for transfers between devices: 29 us -> none  [per_device(): lax.ppermute(p, 'nodes', route(-o))]
    dot_general x2 -> x0, matrix products: 10.8 us -> none  [the longest x1 9.25 us: per_device(): own = jnp.dot(grid_latents, w_keyval, preferred_element_type=jnp.float32)]
    unnamed x14 -> x11, local copies, waits for them, and re-layouts: 0.82 us -> 7.47 us
    ppermute x4 -> x0, starting transfers between devices: 6.56 us -> none  [per_device(): lax.ppermute(p, 'nodes', route(-o))]
    ppermute x4, starting transfers between devices: 7.92 us -> 9.77 us  [per_device(): lax.ppermute(r, 'nodes', route(o))]
  transfers between devices with their start and end apart: 8 -> 4, of which waited for: 2 -> 1; matrix products, arithmetic and copies ran while one was open for 9% -> 3% of each run, Pallas kernels for 0% -> 0%
where the time goes in v3:
time: 68.3 us; the launch traced here: 68 us
  Pallas kernels  45.3 us (66%)
  starting transfers between devices  9.77 us (14%)
  local copies, waits for them, and re-layouts  8.36 us (12%)
  other arithmetic  3.8 us (6%)
  waiting for transfers between devices  0.72 us (1%)
    pallas_call x1, Pallas kernels, encode(): pl.pallas_call(functools.partial(encode_kernel, offsets), out_shape=jax.S...  45.3 us
    ppermute x4, starting transfers between devices, per_device(): lax.ppermute(r, 'nodes', route(o))  9.77 us
    unnamed x11, local copies, waits for them, and re-layouts  7.47 us
  transfers between devices with their start and end apart: 4, of which 1 were waited for; matrix products, arithmetic and copies ran while one was open for 3% of the time, Pallas kernels for 0%

profile of v3, /device:TPU:0, one launch (start us, length us, event | category | flops | bytes accessed | tf_op | source)
XLA Modules:
  0.0 68.0 jit_solution(2171269094559994124)
XLA Ops:
  0.0 0.7 %and_select_fusion.8 = s32[2,6]{1,0:T(2,128)S(1)} fusion(s32[2,6]{1,0:T(2,128)} %param.9), kind=kLoop, calls=%fused_computation.33 | loop fusion | flops 132 | bytes 96 | tf_op jit(solution)/shard_map/jit(remainder)/select_n | solution.py:21
  0.7 0.7 %compare_and_fusion.2 = (pred[2,6]{1,0:T(4,128)(4,1)S(1)}, s32[2,6]{1,0:T(2,128)S(1)}, pred[2,6]{1,0:T(4,128)(4,1)S(1)}) fusion(s32[]{:T(128)S(6)} %axis_index.12, s32[2,6]{1,0:T(2,128)} %param.9, s32[2,6]{1,0:T(2,128)} %live_ref.1), kind=kLoop, calls=%fused_computation.31 | loop fusion | flops 384 | bytes 172 | tf_op jit(solution)/shard_map/and | solution.py:28
  1.4 0.1 copy.11
  1.5 0.1 copy.13
  1.6 0.1 copy.15
  1.7 0.1 copy.8
  1.9 0.1 copy.9
  1.9 0.1 and_reduce_fusion.3
  2.1 0.1 select_reduce_fusion.2
  2.2 0.1 fusion.10
  2.3 0.5 collective-permute-start.1
  2.8 0.1 select_reduce_fusion.1
  2.9 0.1 fusion.11
  3.0 5.6 %collective-permute-start.2 = (s32[2]{0:T(128)S(1)}, s32[2]{0:T(128)S(1)}, u32[]{:S(2)}, u32[]{:S(2)}) collective-permute-start(s32[2]{0:T(128)S(1)} %fusion.11), channel_id=1, source_target_pairs={{0,14},{1,15},{2,0},{3,1},{4,2},{5,3},{6,4},{7,5},{8,6},{9,7},{10,... | collective-permute-start | bytes 32 | tf_op jit(solution)/shard_map/ppermute | solution.py:240
  8.6 0.1 select_reduce_fusion
  8.7 0.1 fusion.12
  8.9 0.1 select_reduce_fusion.3
  9.0 0.1 fusion.9
  9.2 3.6 %collective-permute-start = (s32[2]{0:T(128)S(1)}, s32[2]{0:T(128)S(1)}, u32[]{:S(2)}, u32[]{:S(2)}) collective-permute-start(s32[2]{0:T(128)S(1)} %fusion.9), channel_id=1, source_target_pairs={{0,15},{1,0},{2,1},{3,2},{4,3},{5,4},{6,5},{7,6},{8,7},{9,8},{10,9... | collective-permute-start | bytes 32 | tf_op jit(solution)/shard_map/ppermute | solution.py:240
  12.8 0.5 fusion
  13.4 0.1 copy.17
  13.4 0.1 copy.20
  13.5 0.1 copy.19
  13.7 0.7 %fusion.16.table_ref = s32[2,6]{1,0:T(2,128)S(1)} fusion(s32[2,6]{1,0:T(2,128)S(1)} %get-tuple-element.14, s32[2,6]{1,0:T(2,128)S(1)} %copy.20, s32[2,6]{1,0:T(2,128)S(1)} %copy.19, s32[2,6]{1,0:T(2,128)S(1)} %copy.18, s32[2,6]{1,0:T(2,128)S(1)} %copy.17, pred[2,6]{1,0:T(4,128)(4,1)S(1)} %get-tuple-element.15, s32[2,6]{1,0:T(2,128)} %param.9), kind=kLoop, calls=%fused_computation.48 | loop fusion | flops 348 | bytes 348 | tf_op jit(solution)/shard_map/jit(_where)/select_n | solution.py:36
  14.4 0.7 %collective-permute-done.3 = s32[2]{0:T(128)S(1)} collective-permute-done((s32[2]{0:T(128)S(1)}, s32[2]{0:T(128)S(1)}, u32[]{:S(2)}, u32[]{:S(2)}) %collective-permute-start.3) | collective-permute-done | bytes 40 | tf_op jit(solution)/shard_map/ppermute | solution.py:240
  15.2 1.6 %copy-done = bf16[1024,1024]{1,0:T(8,128)(2,1)S(1)} copy-done((bf16[1024,1024]{1,0:T(8,128)(2,1)S(1)}, bf16[1024,1024]{1,0:T(8,128)(2,1)}, u32[]{:S(2)}) %copy-start) | copy-done | bytes 2097176
  16.8 1.6 %copy-done.1 = bf16[1024,1024]{1,0:T(8,128)(2,1)S(1)} copy-done((bf16[1024,1024]{1,0:T(8,128)(2,1)S(1)}, bf16[1024,1024]{1,0:T(8,128)(2,1)}, u32[]{:S(2)}) %copy-start.1) | copy-done | bytes 2097176
  18.4 1.6 %copy-done.2 = bf16[1024,1024]{1,0:T(8,128)(2,1)S(1)} copy-done((bf16[1024,1024]{1,0:T(8,128)(2,1)S(1)}, bf16[1024,1024]{1,0:T(8,128)(2,1)}, u32[]{:S(2)}) %copy-start.2) | copy-done | bytes 2097176
  20.0 1.0 %copy-done.3 = bf16[256,1024]{1,0:T(8,128)(2,1)S(1)} copy-done((bf16[256,1024]{1,0:T(8,128)(2,1)S(1)}, bf16[256,1024]{1,0:T(8,128)(2,1)}, u32[]{:S(2)}) %copy-start.3) | copy-done | bytes 524312
  21.1 0.7 copy-done.4
  21.7 45.3 %encode.1 = f32[256,1024]{1,0:T(8,128)S(1)} custom-call(s32[8]{0:T(128)S(1)} %pad_add_fusion.request_ref, s32[2,6]{1,0:T(2,128)S(1)} %fusion.16.table_ref, s32[2,6]{1,0:T(2,128)S(1)} %copy-done.4, bf16[8,128,1024]{2,1,0:T(8,128)(2,1)S(1)} %bitcast.1, bf16[256,1024]{1,0:T(8,128)(2,1)S(1)} %copy-done.3, bf16[1024,1024]{1,0:T(8,128)(2,1)S(1)} %copy-done.1, ...), custom_call_target="tpu_custom_call" | custom-call | tf_op jit(solution)/shard_map/encode/pallas_call | solution.py:200
  67.0 1.0 %copy.26 = f32[256,1024]{1,0:T(8,128)} copy(f32[256,1024]{1,0:T(8,128)S(1)} %encode.1) | data formatting | bytes 2097152
  (12 shorter events, 0.2 us)
Async XLA Ops:
  2.3 12.1 %collective-permute-start.1 = (s32[2]{0:T(128)S(1)}, s32[2]{0:T(128)S(1)}, u32[]{:S(2)}, u32[]{:S(2)}) collective-permute-start(s32[2]{0:T(128)S(1)} %fusion.10), channel_id=1, source_target_pairs={{0,1},{1,2},{2,3},{3,4},{4,5},{5,6},{6,7},{7,8},{8,9},{9,10},{10,1... | collective-permute-start | bytes 32 | tf_op jit(solution)/shard_map/ppermute | solution.py:240
  3.0 11.4 %collective-permute-start.2 = (s32[2]{0:T(128)S(1)}, s32[2]{0:T(128)S(1)}, u32[]{:S(2)}, u32[]{:S(2)}) collective-permute-start(s32[2]{0:T(128)S(1)} %fusion.11), channel_id=1, source_target_pairs={{0,14},{1,15},{2,0},{3,1},{4,2},{5,3},{6,4},{7,5},{8,6},{9,7},{10,... | collective-permute-start | bytes 32 | tf_op jit(solution)/shard_map/ppermute | solution.py:240
  8.9 6.3 %collective-permute-start.3 = (s32[2]{0:T(128)S(1)}, s32[2]{0:T(128)S(1)}, u32[]{:S(2)}, u32[]{:S(2)}) collective-permute-start(s32[2]{0:T(128)S(1)} %fusion.12), channel_id=1, source_target_pairs={{0,2},{1,3},{2,4},{3,5},{4,6},{5,7},{6,8},{7,9},{8,10},{9,11},{10,... | collective-permute-start | bytes 32 | tf_op jit(solution)/shard_map/ppermute | solution.py:240
  9.2 6.0 %collective-permute-start = (s32[2]{0:T(128)S(1)}, s32[2]{0:T(128)S(1)}, u32[]{:S(2)}, u32[]{:S(2)}) collective-permute-start(s32[2]{0:T(128)S(1)} %fusion.9), channel_id=1, source_target_pairs={{0,15},{1,0},{2,1},{3,2},{4,3},{5,4},{6,5},{7,6},{8,7},{9,8},{10,9... | collective-permute-start | bytes 32 | tf_op jit(solution)/shard_map/ppermute | solution.py:240
  15.2 1.6 %copy-start = (bf16[1024,1024]{1,0:T(8,128)(2,1)S(1)}, bf16[1024,1024]{1,0:T(8,128)(2,1)}, u32[]{:S(2)}) copy-start(bf16[1024,1024]{1,0:T(8,128)(2,1)} %param.7) | copy-start | bytes 6291460
  16.8 1.6 %copy-start.1 = (bf16[1024,1024]{1,0:T(8,128)(2,1)S(1)}, bf16[1024,1024]{1,0:T(8,128)(2,1)}, u32[]{:S(2)}) copy-start(bf16[1024,1024]{1,0:T(8,128)(2,1)} %w_query_hbm.1) | copy-start | bytes 6291460
  18.4 1.6 %copy-start.2 = (bf16[1024,1024]{1,0:T(8,128)(2,1)S(1)}, bf16[1024,1024]{1,0:T(8,128)(2,1)}, u32[]{:S(2)}) copy-start(bf16[1024,1024]{1,0:T(8,128)(2,1)} %w_out_hbm.1) | copy-start | bytes 6291460
  20.0 1.0 %copy-start.3 = (bf16[256,1024]{1,0:T(8,128)(2,1)S(1)}, bf16[256,1024]{1,0:T(8,128)(2,1)}, u32[]{:S(2)}) copy-start(bf16[256,1024]{1,0:T(8,128)(2,1)} %mesh_ref.1) | copy-start | bytes 1572868
  21.1 0.7 copy-start.4

commit v4 on v3

--- a/solution.py
+++ b/solution.py
@@ -13,7 +13,7 @@
 CAP = 2
 GROUP = 4
 CHUNK = 256
-VMEM_LIMIT = 44 * 1024 * 1024
+VMEM_LIMIT = 60 * 1024 * 1024
 
 
 def plan_requests(tiles, live, own_tiles, offsets, position, node_count):
@@ -71,9 +71,14 @@
     w_query_ref,
     w_keyval_ref,
     w_out_ref,
+    asked_ref,
+    asked_smem,
     weight_sems,
     send_sems,
     recv_sems,
+    ask_send_sems,
+    ask_recv_sems,
+    ask_sems,
 ):
     own_tiles, tile_rows, width = grid_ref.shape
     head_size = width // HEADS
@@ -84,8 +89,8 @@
         pltpu.make_async_copy(source, target, weight_sems.at[number])
         for number, (source, target) in enumerate(
             (
+                (w_query_hbm, w_query_ref),
                 (w_keyval_hbm, w_keyval_ref),
-                (w_query_hbm, w_query_ref),
                 (w_out_hbm, w_out_ref),
             )
         )
@@ -103,10 +108,36 @@
         )
     pl.semaphore_wait(barrier, len(offsets))
 
+    asks = []
+    for number, offset in enumerate(offsets):
+        ask = pltpu.make_async_remote_copy(
+            src_ref=request_ref.at[number],
+            dst_ref=asked_ref.at[number],
+            send_sem=ask_send_sems.at[number],
+            recv_sem=ask_recv_sems.at[number],
+            device_id={"nodes": shifted(offset)},
+            device_id_type=pl.DeviceIdType.MESH,
+        )
+        ask.start()
+        asks.append(ask)
+
+    loads[0].wait()
+
+    def store_query(columns, done):
+        query_ref[:, columns] = (done * head_size ** (-0.5)).astype(query_ref.dtype)
+
+    project(lambda: mesh_ref[...], w_query_ref, store_query)
+
     copies = []
     for number, offset in enumerate(offsets):
+        asks[number].wait()
+        fetch = pltpu.make_async_copy(
+            asked_ref.at[number], asked_smem.at[number], ask_sems.at[number]
+        )
+        fetch.start()
+        fetch.wait()
         for slot in range(CAP):
-            sending[number, slot] = grid_ref[request_ref[number * CAP + slot]]
+            sending[number, slot] = grid_ref[asked_smem[number, 0, slot]]
         copy = pltpu.make_async_remote_copy(
             src_ref=sending.at[number],
             dst_ref=received.at[number],
@@ -126,21 +157,15 @@
 
         return store
 
-    loads[0].wait()
+    loads[1].wait()
     project(
         lambda: grid_ref[...].reshape(own_tiles * tile_rows, width),
         w_keyval_ref,
         keep(0, own_tiles),
     )
-    loads[1].wait()
-
-    def store_query(columns, done):
-        query_ref[:, columns] = (done * head_size ** (-0.5)).astype(query_ref.dtype)
-
-    project(lambda: mesh_ref[...], w_query_ref, store_query)
     loads[2].wait()
 
-    pair = 2
+    pair = 1
     for first in range(0, len(offsets), pair):
         for copy in copies[first : first + pair]:
             copy.wait()
@@ -200,7 +225,7 @@
     return pl.pallas_call(
         functools.partial(encode_kernel, offsets),
         out_shape=jax.ShapeDtypeStruct(mesh_latents.shape, jnp.float32),
-        in_specs=[smem, smem, smem, vmem, vmem, hbm, hbm, hbm],
+        in_specs=[vmem, smem, smem, vmem, vmem, hbm, hbm, hbm],
         out_specs=vmem,
         scratch_shapes=[
             pltpu.VMEM((own_tiles + count * CAP, tile_rows, 2 * width), bf16),
@@ -211,7 +236,12 @@
             pltpu.VMEM(w_query.shape, bf16),
             pltpu.VMEM(w_keyval.shape, bf16),
             pltpu.VMEM(w_out.shape, bf16),
+            pltpu.VMEM(request.shape, jnp.int32),
+            pltpu.SMEM(request.shape, jnp.int32),
             pltpu.SemaphoreType.DMA((3,)),
+            pltpu.SemaphoreType.DMA((count,)),
+            pltpu.SemaphoreType.DMA((count,)),
+            pltpu.SemaphoreType.DMA((count,)),
             pltpu.SemaphoreType.DMA((count,)),
             pltpu.SemaphoreType.DMA((count,)),
         ],
@@ -231,16 +261,13 @@
     position = lax.axis_index("nodes")
     offsets = [sign * o for o in range(1, REACH + 1) for sign in (-1, 1)]
 
-    def route(shift):
-        return [(i, (i + shift) % node_count) for i in range(node_count)]
-
     requests, table = plan_requests(
         neighbour_tiles, neighbour_live, own_tiles, offsets, position, node_count
     )
-    asked = [lax.ppermute(r, "nodes", route(o)) for r, o in zip(requests, offsets)]
+    request = jnp.pad(jnp.stack(requests)[:, None, :], ((0, 0), (0, 7), (0, 128 - CAP)))
     return encode(
         offsets,
-        jnp.concatenate(asked),
+        request,
         table,
         neighbour_live,
         grid_latents.reshape(own_tiles, TILE, width),

time: 68.3 us -> 63.8 us (0.934)
  Pallas kernels: 45.3 us -> 55.6 us
  starting transfers between devices: 9.77 us -> 0 us
  local copies, waits for them, and re-layouts: 8.36 us -> 3.81 us
  waiting for transfers between devices: 0.72 us -> 0 us
    pallas_call x1, Pallas kernels: 45.3 us -> 55.6 us  [encode(): pl.pallas_call(functools.partial(encode_kernel, offsets), out_shape=jax.S...]
    ppermute x4 -> x0, starting transfers between devices: 9.77 us -> none  [per_device(): lax.ppermute(r, 'nodes', route(o))]
    unnamed x11 -> x1, local copies, waits for them, and re-layouts: 7.47 us -> 2.31 us
    ppermute x4 -> x0, waiting for transfers between devices: 0.72 us -> none  [per_device(): lax.ppermute(r, 'nodes', route(o))]
  transfers between devices with their start and end apart: 4 -> 0, of which waited for: 1 -> 0; matrix products, arithmetic and copies ran while one was open for 3% -> 0% of each run, Pallas kernels for 0% -> 0%
where the time goes in v4:
time: 63.8 us; the launch traced here: 63.6 us
  Pallas kernels  55.6 us (87%)
  other arithmetic  4.15 us (7%)
  local copies, waits for them, and re-layouts  3.81 us (6%)
    pallas_call x1, Pallas kernels, encode(): pl.pallas_call(functools.partial(encode_kernel, offsets), out_shape=jax.S...  55.6 us
    unnamed x1, local copies, waits for them, and re-layouts  2.31 us
    select_n x1, other arithmetic, plan_requests(): table = jnp.where(wanted, own_tiles + number * CAP + place, table)  1.28 us

profile of v4, /device:TPU:0, one launch (start us, length us, event | category | flops | bytes accessed | tf_op | source)
XLA Modules:
  0.0 63.6 jit_solution(11026869828816444815)
XLA Ops:
  0.0 0.7 %and_select_fusion.8 = s32[2,6]{1,0:T(2,128)S(1)} fusion(s32[2,6]{1,0:T(2,128)} %param.9), kind=kLoop, calls=%fused_computation.34 | loop fusion | flops 132 | bytes 96 | tf_op jit(solution)/shard_map/jit(remainder)/select_n | solution.py:21
  0.7 0.7 %compare_and_fusion.2 = (pred[2,6]{1,0:T(4,128)(4,1)S(1)}, s32[2,6]{1,0:T(2,128)S(1)}, pred[2,6]{1,0:T(4,128)(4,1)S(1)}) fusion(s32[]{:T(128)S(6)} %axis_index.12, s32[2,6]{1,0:T(2,128)} %param.9, s32[2,6]{1,0:T(2,128)} %live_ref.1), kind=kLoop, calls=%fused_computation.32 | loop fusion | flops 384 | bytes 172 | tf_op jit(solution)/shard_map/and | solution.py:28
  1.4 0.1 copy.13
  1.5 0.1 copy.15
  1.6 0.1 copy.17
  1.7 0.1 copy.10
  1.9 0.1 copy.11
  1.9 0.1 and_reduce_fusion.3
  2.1 0.1 select_reduce_fusion.2
  2.2 0.1 fusion.10
  2.3 0.1 fusion.9
  2.5 0.2 select_reduce_fusion
  2.6 0.1 fusion.12
  2.7 0.1 fusion.11
  2.9 0.6 fusion
  3.4 0.1 copy.21
  3.5 0.1 copy.24
  3.6 0.1 copy.23
  3.7 0.1 copy.22
  3.8 1.3 %fusion.16.table_ref = s32[2,6]{1,0:T(2,128)} fusion(s32[2,6]{1,0:T(2,128)S(1)} %get-tuple-element.14, s32[2,6]{1,0:T(2,128)S(1)} %copy.24, s32[2,6]{1,0:T(2,128)S(1)} %copy.23, s32[2,6]{1,0:T(2,128)S(1)} %copy.22, s32[2,6]{1,0:T(2,128)S(1)} %copy.21, pred[2,6]{1,0:T(4,128)(4,1)S(1)} %get-tuple-element.15, s32[2,6]{1,0:T(2,128)} %param.9), kind=kLoop, calls=%fused_computation.49 | loop fusion | flops 348 | bytes 348 | tf_op jit(solution)/shard_map/jit(_where)/select_n | solution.py:36
  5.1 0.6 pad.4.request_ref
  5.7 55.6 %encode.1 = f32[256,1024]{1,0:T(8,128)} custom-call(s32[4,8,128]{2,1,0:T(8,128)} %pad.4.request_ref, s32[2,6]{1,0:T(2,128)} %fusion.16.table_ref, s32[2,6]{1,0:T(2,128)} %live_ref.1, bf16[8,128,1024]{2,1,0:T(8,128)(2,1)} %bitcast.8, bf16[256,1024]{1,0:T(8,128)(2,1)} %mesh_ref.1, bf16[1024,1024]{1,0:T(8,128)(2,1)} %w_query_hbm.1, ...), custom_call_target="tpu_custom_call" | custom-call | tf_op jit(solution)/shard_map/encode/pallas_call | solution.py:225
  61.3 2.3 %copy.32 = f32[256,1024]{1,0:T(8,128)} copy(f32[256,1024]{1,0:T(8,128)} %encode.1) | data formatting | bytes 2097152
  (2 shorter events, 0.0 us)

commit v5 on v4

--- a/solution.py
+++ b/solution.py
@@ -13,7 +13,7 @@
 CAP = 2
 GROUP = 4
 CHUNK = 256
-VMEM_LIMIT = 60 * 1024 * 1024
+VMEM_LIMIT = 52 * 1024 * 1024
 
 
 def plan_requests(tiles, live, own_tiles, offsets, position, node_count):
@@ -128,14 +128,18 @@
 
     project(lambda: mesh_ref[...], w_query_ref, store_query)
 
+    fetches = []
+    for number, ask in enumerate(asks):
+        ask.wait()
+        fetch = pltpu.make_async_copy(
+            asked_ref.at[number], asked_smem.at[number], ask_sems.at[number]
+        )
+        fetch.start()
+        fetches.append(fetch)
+
     copies = []
     for number, offset in enumerate(offsets):
-        asks[number].wait()
-        fetch = pltpu.make_async_copy(
-            asked_ref.at[number], asked_smem.at[number], ask_sems.at[number]
-        )
-        fetch.start()
-        fetch.wait()
+        fetches[number].wait()
         for slot in range(CAP):
             sending[number, slot] = grid_ref[asked_smem[number, 0, slot]]
         copy = pltpu.make_async_remote_copy(

time: 63.8 us -> 61.5 us (0.964)
  Pallas kernels: 55.6 us -> 53.9 us
    pallas_call x1, Pallas kernels: 55.6 us -> 53.9 us  [encode(): pl.pallas_call(functools.partial(encode_kernel, offsets), out_shape=jax.S...]
    unnamed x1 -> x5, local copies, waits for them, and re-layouts: 2.31 us -> 2.69 us
where the time goes in v5:
time: 61.5 us; the launch traced here: 61.2 us
  Pallas kernels  53.9 us (88%)
  local copies, waits for them, and re-layouts  3.59 us (6%)
  other arithmetic  3.56 us (6%)
    pallas_call x1, Pallas kernels, encode(): pl.pallas_call(functools.partial(encode_kernel, offsets), out_shape=jax.S...  53.9 us
    unnamed x5, local copies, waits for them, and re-layouts  2.69 us

profile of v5, /device:TPU:0, one launch (start us, length us, event | category | flops | bytes accessed | tf_op | source)
XLA Modules:
  0.0 61.2 jit_solution(15741690165393069170)
XLA Ops:
  0.0 0.7 %and_select_fusion.8 = s32[2,6]{1,0:T(2,128)S(1)} fusion(s32[2,6]{1,0:T(2,128)} %param.9), kind=kLoop, calls=%fused_computation.34 | loop fusion | flops 132 | bytes 96 | tf_op jit(solution)/shard_map/jit(remainder)/select_n | solution.py:21
  0.7 0.7 %compare_and_fusion.2 = (pred[2,6]{1,0:T(4,128)(4,1)S(1)}, s32[2,6]{1,0:T(2,128)S(1)}, pred[2,6]{1,0:T(4,128)(4,1)S(1)}) fusion(s32[]{:T(128)S(6)} %axis_index.12, s32[2,6]{1,0:T(2,128)} %param.9, s32[2,6]{1,0:T(2,128)} %live_ref.1), kind=kLoop, calls=%fused_computation.32 | loop fusion | flops 384 | bytes 172 | tf_op jit(solution)/shard_map/and | solution.py:28
  1.4 0.1 copy.13
  1.5 0.1 copy.15
  1.6 0.1 copy.17
  1.7 0.1 copy.10
  1.9 0.1 copy.11
  1.9 0.1 and_reduce_fusion.3
  2.1 0.1 select_reduce_fusion.2
  2.2 0.1 fusion.10
  2.3 0.1 fusion.9
  2.5 0.2 select_reduce_fusion
  2.6 0.1 fusion.12
  2.7 0.1 fusion.11
  2.9 0.6 fusion
  3.4 0.1 copy.21
  3.5 0.1 copy.24
  3.6 0.1 copy.23
  3.7 0.1 copy.22
  3.8 0.7 %fusion.16.table_ref = s32[2,6]{1,0:T(2,128)S(1)} fusion(s32[2,6]{1,0:T(2,128)S(1)} %get-tuple-element.14, s32[2,6]{1,0:T(2,128)S(1)} %copy.24, s32[2,6]{1,0:T(2,128)S(1)} %copy.23, s32[2,6]{1,0:T(2,128)S(1)} %copy.22, s32[2,6]{1,0:T(2,128)S(1)} %copy.21, pred[2,6]{1,0:T(4,128)(4,1)S(1)} %get-tuple-element.15, s32[2,6]{1,0:T(2,128)} %param.9), kind=kLoop, calls=%fused_computation.49 | loop fusion | flops 348 | bytes 348 | tf_op jit(solution)/shard_map/jit(_where)/select_n | solution.py:36
  4.5 0.0 copy-start
  4.5 1.0 %copy-done = bf16[256,1024]{1,0:T(8,128)(2,1)S(1)} copy-done((bf16[256,1024]{1,0:T(8,128)(2,1)S(1)}, bf16[256,1024]{1,0:T(8,128)(2,1)}, u32[]{:S(2)}) %copy-start) | copy-done | bytes 524312
  5.6 0.0 copy-start.1
  5.6 0.7 %copy-done.1 = s32[2,6]{1,0:T(2,128)S(1)} copy-done((s32[2,6]{1,0:T(2,128)S(1)}, s32[2,6]{1,0:T(2,128)}, u32[]{:S(2)}) %copy-start.1) | copy-done | bytes 72
  6.2 53.9 %encode.1 = f32[256,1024]{1,0:T(8,128)S(1)} custom-call(s32[4,8,128]{2,1,0:T(8,128)S(1)} %pad.4.request_ref, s32[2,6]{1,0:T(2,128)S(1)} %fusion.16.table_ref, s32[2,6]{1,0:T(2,128)S(1)} %copy-done.1, bf16[8,128,1024]{2,1,0:T(8,128)(2,1)} %bitcast.8, bf16[256,1024]{1,0:T(8,128)(2,1)S(1)} %copy-done, bf16[1024,1024]{1,0:T(8,128)(2,1)} %w_query_hbm.1, ...), custom_call_target="tpu_custom_call" | custom-call | tf_op jit(solution)/shard_map/encode/pallas_call | solution.py:229
  60.2 1.0 %copy.32 = f32[256,1024]{1,0:T(8,128)} copy(f32[256,1024]{1,0:T(8,128)S(1)} %encode.1) | data formatting | bytes 2097152
  (3 shorter events, 0.0 us)
Async XLA Ops:
  4.5 1.0 %copy-start = (bf16[256,1024]{1,0:T(8,128)(2,1)S(1)}, bf16[256,1024]{1,0:T(8,128)(2,1)}, u32[]{:S(2)}) copy-start(bf16[256,1024]{1,0:T(8,128)(2,1)} %mesh_ref.1) | copy-start | bytes 1572868
  5.6 0.7 %copy-start.1 = (s32[2,6]{1,0:T(2,128)S(1)}, s32[2,6]{1,0:T(2,128)}, u32[]{:S(2)}) copy-start(s32[2,6]{1,0:T(2,128)} %live_ref.1) | copy-start | bytes 148
